TPU v7x, 768 devices: a whole 4x8x12 slice. The times are simulated.
768 devices in a mesh: mesh: 96 (over x, z, core), lev: 8 (over y).
Axes of the slice: x: 4, y: 8, z: 12, core: 2. Of those that a mesh axis runs over, the one named last changes fastest.
Arguments:
- velocity: float32 [16, 294912], P('lev', 'mesh'), may hold values from -6 to 6
- thickness: float32 [16, 294912], P('lev', 'mesh'), may hold values from 0.5 to 2
- vorticity: float32 [16, 294912], P('lev', 'mesh'), may hold values from -6 to 6
- vertical_wind: float32 [16, 294912], P('lev', 'mesh'), may hold values from -6 to 6
- weights_on_edge: float32 [10, 294912], P(None, 'mesh'), may hold values from -2 to 2
- edges_on_edge: int32 [10, 294912], P(None, 'mesh'), may hold values from 0 to 3839, as said below
- edges_on_cell: int32 [6, 98304], P(None, 'mesh'), may hold values from 0 to 3839, as said below
- cells_on_edge: int32 [2, 294912], P(None, 'mesh'), may hold values from 0 to 1407, as said below
- energy_weight: float32 [6, 98304], P(None, 'mesh'), may hold values from 0.05 to 0.5
- inverse_distance: float32 [294912], P('mesh'), may hold values from 0.5 to 2
- edge_halo_list: int32 [576, 128], P('mesh'), may hold values from 0 to 3071
- edge_halo_count: int32 [576], P('mesh'), may hold values from 1 to 128, as said below
- cell_halo_list: int32 [576, 64], P('mesh'), may hold values from 0 to 1023
- cell_halo_count: int32 [576], P('mesh'), may hold values from 1 to 64, as said below
Outputs:
- tendency: float32 [16, 294912], P('lev', 'mesh')
- tangent: float32 [16, 294912], P('lev', 'mesh')
- energy: float32 [16, 98304], P('lev', 'mesh')
Inputs may be any that keep to these rules, and one draw needn't show every extreme that they name: `edge_halo_count`: row r names how many leading slots of the halo block r are live. `cell_halo_count`: row r names how many leading slots of the halo block r are live. `edges_on_edge`: entries name local edges or live slots of edge halo blocks. `edges_on_cell`: entries name local edges or live slots of edge halo blocks. `cells_on_edge`: entries name local cells or live slots of cell halo blocks.
All inputs are finite; a program needn't handle non-finite values.
Results may differ from a plain program's by a relative error of at most 0.0003.
Values sent between devices are 32-bit elements; how exact they have to be, the bound alone decides.
No kernel may reach another device: no remote copies, remote signals or barrier semaphores. Data moves between devices by JAX's collectives and lax.ppermute only.
A program may use at most 128 MiB of HBM per device.

v0:
```python
import jax
import jax.numpy as jnp
from jax import lax
from jax.sharding import PartitionSpec as P

REACH = 3


def from_behind(block, axis, distance):
    devices = range(lax.axis_size(axis))
    route = [((i - distance) % len(devices), i) for i in devices]
    return lax.ppermute(block, axis, route)


def padded(block, sides, width):
    for axis, dim in sides:
        count = lax.axis_size(axis)
        forward = [(i, i + 1) for i in range(count - 1)]
        backward = [(target, source) for source, target in forward]
        low = lax.ppermute(
            lax.slice_in_dim(block, block.shape[dim] - width, None, axis=dim), axis, forward
        )
        high = lax.ppermute(lax.slice_in_dim(block, 0, width, axis=dim), axis, backward)
        block = jnp.concatenate([low, block, high], axis=dim)
    return block


def pack_blocks(fields, halo_list, halo_count):
    breadth = halo_list.shape[1]
    picked = jnp.take(fields, halo_list.reshape(-1), axis=2)
    picked = picked.reshape(fields.shape[0], fields.shape[1], halo_list.shape[0], breadth)
    living = jnp.arange(breadth)[None, :] < halo_count[:, None]
    return jnp.where(living[None, None], picked, 0.0)


def route_edges(blocks):
    pieces = []
    for block_index in range(2 * REACH):
        offset = block_index + 1 if block_index < REACH else REACH - 1 - block_index
        pieces.append(from_behind(blocks[:, :, block_index, :], "mesh", offset))
    return jnp.stack(pieces, axis=2)


def route_cells(blocks):
    pieces = []
    for block_index in range(2 * REACH):
        offset = block_index + 1 if block_index < REACH else REACH - 1 - block_index
        pieces.append(from_behind(blocks[:, :, block_index, :], "mesh", offset))
    return jnp.stack(pieces, axis=2)


def lookup(field, table):
    return jnp.take(field, table.reshape(-1), axis=1).reshape(
        field.shape[0], table.shape[0], table.shape[1]
    )


def body(
    velocity,
    thickness,
    vorticity,
    vertical_wind,
    weights_on_edge,
    edges_on_edge,
    edges_on_cell,
    cells_on_edge,
    energy_weight,
    inverse_distance,
    edge_halo_list,
    edge_halo_count,
    cell_halo_list,
    cell_halo_count,
):
    levels, edge_total = velocity.shape
    fields = jnp.stack([velocity, thickness, vorticity])
    received = route_edges(pack_blocks(fields, edge_halo_list, edge_halo_count))
    extended = jnp.concatenate([fields, received.reshape(3, levels, -1)], axis=2)
    speed_near = lookup(extended[0], edges_on_edge)
    tangent = jnp.sum(weights_on_edge * speed_near, axis=1)
    height_near = lookup(extended[1], edges_on_edge)
    moved = weights_on_edge * speed_near * height_near
    potential_near = lookup(extended[2], edges_on_edge)
    flux = jnp.sum(moved * 0.5 * (vorticity[:, None, :] + potential_near), axis=1)
    cell_speed = lookup(extended[0], edges_on_cell)
    energy = jnp.sum(energy_weight * cell_speed * cell_speed, axis=1)
    cell_received = route_cells(pack_blocks(energy[None], cell_halo_list, cell_halo_count))
    cell_extended = jnp.concatenate([energy, cell_received[0].reshape(levels, -1)], axis=1)
    ends = lookup(cell_extended, cells_on_edge)
    gradient = (ends[:, 1] - ends[:, 0]) * inverse_distance
    rims = padded(velocity, (("lev", 0),), 1)
    advect = -0.5 * vertical_wind * (rims[2:] - rims[:-2])
    tendency = flux - gradient + advect
    return (tendency, tangent, energy)


def solution(mesh):
    in_specs = (
        P("lev", "mesh"),
        P("lev", "mesh"),
        P("lev", "mesh"),
        P("lev", "mesh"),
        P(None, "mesh"),
        P(None, "mesh"),
        P(None, "mesh"),
        P(None, "mesh"),
        P(None, "mesh"),
        P("mesh"),
        P("mesh", None),
        P("mesh"),
        P("mesh", None),
        P("mesh"),
    )
    out_specs = (P("lev", "mesh"), P("lev", "mesh"), P("lev", "mesh"))
    return jax.shard_map(body, mesh=mesh, in_specs=in_specs, out_specs=out_specs, check_vma=False)
```

profile of v0, /device:TPU:1, one launch (start us, length us, event | category | flops | bytes accessed | tf_op | source)
XLA Modules:
  0.0 565.1 jit_solution(13800373959652287463)
XLA Ops:
  0.6 1.4 fusion.10
  2.1 1.3 collective-permute-start.12
  3.4 5.3 collective-permute-start.13
  10.9 0.8 pad_maximum_fusion.2
  11.7 2.9 copy.166
  14.6 3.2 gather_fusion
  17.9 1.3 copy.167
  19.2 17.8 %collective-permute-start.5 = (f32[3,2,128]{2,1,0:T(2,128)S(1)}, f32[3,2,128]{2,1,0:T(2,128)S(1)}, u32[]{:S(2)}, u32[]{:S(2)}) collective-permute-start(f32[3,2,128]{2,1,0:T(2,128)S(1)} %get-tuple-element.41), channel_id=1, source_target_pairs={{24,0},{32,8},{40,16},{48,24},{56,32},{64,40},{72,48},{80,56},{88,... | collective-permute-start | bytes 9224 | tf_op jit(solution)/shard_map/ppermute | solution.py:12
  37.0 2.2 collective-permute-start.4
  39.2 2.5 collective-permute-start
  41.7 1.0 reshape.267
  44.0 1.4 compare_and_fusion.2
  48.4 1.4 iota_compare_fusion
  49.7 1.2 copy.175
  51.0 3.1 collective-permute-start.1
  54.1 4.5 collective-permute-done.1
  58.7 1.9 collective-permute-start.2
  60.6 6.3 %collective-permute-done.2 = f32[3,2,128]{2,1,0:T(2,128)S(1)} collective-permute-done((f32[3,2,128]{2,1,0:T(2,128)S(1)}, f32[3,2,128]{2,1,0:T(2,128)S(1)}, u32[]{:S(2)}, u32[]{:S(2)}) %collective-permute-start.2) | collective-permute-done | bytes 3104 | tf_op jit(solution)/shard_map/ppermute | solution.py:12
  66.9 3.8 collective-permute-start.3
  70.7 1.1 collective-permute-done.3
  71.8 0.8 pad_maximum_fusion.1
  73.3 1.9 copy.174
  75.2 1.3 copy.173
  76.5 2.6 copy.176
  79.2 22.9 %gather_fusion.1 = f32[6144,2]{1,0:T(8,128)} fusion(f32[2,3840]{0,1:T(8,128)S(1)} %copy.173, s32[6144]{0:T(1024)} %get-tuple-element.54), kind=kCustom, calls=%fused_computation.4 | custom fusion | bytes 122880 | tf_op jit(solution)/shard_map/jit(_take)/gather | solution.py:53
  102.1 5.5 fusion
  107.6 1.8 copy.185
  109.4 2.6 gather_fusion.2
  112.1 1.6 copy.178
  115.0 1.9 collective-permute-start.11
  117.0 6.8 %collective-permute-start.10 = (f32[1,2,64]{2,1,0:T(2,128)}, f32[1,2,64]{2,1,0:T(2,128)}, u32[]{:S(2)}, u32[]{:S(2)}) collective-permute-start(f32[1,2,64]{2,1,0:T(2,128)} %get-tuple-element.48), channel_id=1, source_target_pairs={{16,0},{24,8},{32,16},{40,24},{48,32},{56,40},{64,48},{72,56},{80,... | collective-permute-start | bytes 1544 | tf_op jit(solution)/shard_map/ppermute | solution.py:12
  123.8 3.4 collective-permute-start.6
  127.1 111.5 %gather_fusion.4 = f32[30720,2]{1,0:T(8,128)} fusion(f32[2,3840]{0,1:T(8,128)S(1)} %copy.173, s32[30720]{0:T(1024)} %fusion.1), kind=kCustom, calls=%fused_computation.clone | custom fusion | bytes 614400 | tf_op jit(solution)/shard_map/jit(_take)/gather | solution.py:53
  238.6 113.0 %gather_fusion.6 = f32[30720,2]{1,0:T(8,128)} fusion(f32[2,3840]{0,1:T(8,128)} %copy.176, s32[30720]{0:T(1024)} %fusion.1), kind=kCustom, calls=%fused_computation.2.clone | custom fusion | bytes 614400 | tf_op jit(solution)/shard_map/jit(_take)/gather | solution.py:53
  351.6 113.0 %gather_fusion.5 = f32[30720,2]{1,0:T(8,128)} fusion(f32[2,3840]{0,1:T(8,128)} %copy.174, s32[30720]{0:T(1024)} %fusion.1), kind=kCustom, calls=%fused_computation.1.clone | custom fusion | bytes 614400 | tf_op jit(solution)/shard_map/jit(_take)/gather | solution.py:53
  464.7 32.9 %broadcast_select_fusion.1 = (f32[30720,2]{1,0:T(8,128)}, f32[30720,2]{1,0:T(8,128)}, f32[30720,2]{1,0:T(8,128)}) fusion(f32[30720,2]{1,0:T(8,128)} %gather_fusion.5, pred[30720]{0:T(1024)(128)(4,1)} %compare_and_fusion, f32[30720,2]{1,0:T(8,128)} %gather_fusion.6, f32[30720,2]{1,0:T(8,128)} %gather_fusion.4), kind=kLoop, calls=%fused_computation.10 | loop fusion | flops 184320 | bytes 1505280 | tf_op jit(solution)/shard_map/jit(_take)/select_n | solution.py:53
  497.6 17.2 %multiply_reduce_fusion.1 = (f32[2,3072]{0,1:T(8,128)}, f32[2,3072]{0,1:T(8,128)S(1)}) fusion(f32[2,10,3072]{0,2,1:T(8,128)} %bitcast.115, f32[10,3072]{1,0:T(8,128)S(1)} %copy-done, f32[2,10,3072]{0,2,1:T(8,128)} %bitcast.114, f32[2,3072]{0,1:T(8,128)S(1)} %copy.175, f32[2,10,3072]{0,2,1:T(8,128)} %bitcast.113), kind=kLoop, calls=%fused_computation.8 | loop fusion | flops 417792 | bytes 933888 | tf_op jit(solution)/shard_map/reduce_sum | solution.py:79
  514.8 2.5 copy.184
  517.7 3.6 collective-permute-start.7
  522.0 3.3 collective-permute-done.7
  525.4 1.9 collective-permute-start.8
  527.3 6.6 %collective-permute-done.8 = f32[1,2,64]{2,1,0:T(2,128)S(1)} collective-permute-done((f32[1,2,64]{2,1,0:T(2,128)S(1)}, f32[1,2,64]{2,1,0:T(2,128)S(1)}, u32[]{:S(2)}, u32[]{:S(2)}) %collective-permute-start.8) | collective-permute-done | bytes 544 | tf_op jit(solution)/shard_map/ppermute | solution.py:12
  533.9 2.7 collective-permute-start.9
  536.6 2.2 collective-permute-done.9
  540.2 2.0 pad_maximum_fusion
  542.2 20.1 %gather_fusion.3 = f32[6144,2]{1,0:T(8,128)S(1)} fusion(f32[2,1408]{0,1:T(8,128)} %pad_maximum_fusion, s32[6144]{0:T(1024)} %get-tuple-element.53), kind=kCustom, calls=%fused_computation.6 | custom fusion | bytes 122880 | tf_op jit(solution)/shard_map/jit(_take)/gather | solution.py:53
  562.3 1.2 copy.182
  563.6 1.5 fusion.4
  (49 shorter events, 11.3 us)
Async XLA Ops:
  2.1 561.5 %collective-permute-start.12 = (f32[1,3072]{1,0:T(1,128)}, f32[1,3072]{1,0:T(1,128)}, u32[]{:S(2)}, u32[]{:S(2)}) collective-permute-start(f32[1,3072]{1,0:T(1,128)} %get-tuple-element.39), channel_id=1, source_target_pairs={{1,0},{2,1},{3,2},{4,3},{5,4},{6,5},{7,6},{9,8},{10,9},{11,10},{12... | collective-permute-start | bytes 36872 | tf_op jit(solution)/shard_map/ppermute | solution.py:23
  3.4 560.2 %collective-permute-start.13 = (f32[1,3072]{1,0:T(1,128)}, f32[1,3072]{1,0:T(1,128)}, u32[]{:S(2)}, u32[]{:S(2)}) collective-permute-start(f32[1,3072]{1,0:T(1,128)} %get-tuple-element.40), channel_id=1, source_target_pairs={{0,1},{1,2},{2,3},{3,4},{4,5},{5,6},{6,7},{8,9},{9,10},{10,11},{11... | collective-permute-start | bytes 36872 | tf_op jit(solution)/shard_map/ppermute | solution.py:20
  19.2 52.6 %collective-permute-start.5 = (f32[3,2,128]{2,1,0:T(2,128)S(1)}, f32[3,2,128]{2,1,0:T(2,128)S(1)}, u32[]{:S(2)}, u32[]{:S(2)}) collective-permute-start(f32[3,2,128]{2,1,0:T(2,128)S(1)} %get-tuple-element.41), channel_id=1, source_target_pairs={{24,0},{32,8},{40,16},{48,24},{56,32},{64,40},{72,48},{80,56},{88,... | collective-permute-start | bytes 9224 | tf_op jit(solution)/shard_map/ppermute | solution.py:12
  37.0 34.8 %collective-permute-start.4 = (f32[3,2,128]{2,1,0:T(2,128)S(1)}, f32[3,2,128]{2,1,0:T(2,128)S(1)}, u32[]{:S(2)}, u32[]{:S(2)}) collective-permute-start(f32[3,2,128]{2,1,0:T(2,128)S(1)} %get-tuple-element.42), channel_id=1, source_target_pairs={{16,0},{24,8},{32,16},{40,24},{48,32},{56,40},{64,48},{72,56},{80,... | collective-permute-start | bytes 9224 | tf_op jit(solution)/shard_map/ppermute | solution.py:12
  39.2 11.8 %collective-permute-start = (f32[3,2,128]{2,1,0:T(2,128)S(1)}, f32[3,2,128]{2,1,0:T(2,128)S(1)}, u32[]{:S(2)}, u32[]{:S(2)}) collective-permute-start(f32[3,2,128]{2,1,0:T(2,128)S(1)} %get-tuple-element.46), channel_id=1, source_target_pairs={{760,0},{0,8},{8,16},{16,24},{24,32},{32,40},{40,48},{48,56},{56,6... | collective-permute-start | bytes 9224 | tf_op jit(solution)/shard_map/ppermute | solution.py:12
  51.0 7.7 %collective-permute-start.1 = (f32[3,2,128]{2,1,0:T(2,128)S(1)}, f32[3,2,128]{2,1,0:T(2,128)S(1)}, u32[]{:S(2)}, u32[]{:S(2)}) collective-permute-start(f32[3,2,128]{2,1,0:T(2,128)S(1)} %get-tuple-element.45), channel_id=1, source_target_pairs={{752,0},{760,8},{0,16},{8,24},{16,32},{24,40},{32,48},{40,56},{48,... | collective-permute-start | bytes 9224 | tf_op jit(solution)/shard_map/ppermute | solution.py:12
  58.7 8.2 %collective-permute-start.2 = (f32[3,2,128]{2,1,0:T(2,128)S(1)}, f32[3,2,128]{2,1,0:T(2,128)S(1)}, u32[]{:S(2)}, u32[]{:S(2)}) collective-permute-start(f32[3,2,128]{2,1,0:T(2,128)S(1)} %get-tuple-element.44), channel_id=1, source_target_pairs={{744,0},{752,8},{760,16},{0,24},{8,32},{16,40},{24,48},{32,56},{40... | collective-permute-start | bytes 9224 | tf_op jit(solution)/shard_map/ppermute | solution.py:12
  66.9 4.9 collective-permute-start.3
  115.0 424.4 %collective-permute-start.11 = (f32[1,2,64]{2,1,0:T(2,128)S(1)}, f32[1,2,64]{2,1,0:T(2,128)}, u32[]{:S(2)}, u32[]{:S(2)}) collective-permute-start(f32[1,2,64]{2,1,0:T(2,128)S(1)} %get-tuple-element.47), channel_id=1, source_target_pairs={{24,0},{32,8},{40,16},{48,24},{56,32},{64,40},{72,48},{80,56},{88,... | collective-permute-start | bytes 1544 | tf_op jit(solution)/shard_map/ppermute | solution.py:12
  117.0 421.8 %collective-permute-start.10 = (f32[1,2,64]{2,1,0:T(2,128)}, f32[1,2,64]{2,1,0:T(2,128)}, u32[]{:S(2)}, u32[]{:S(2)}) collective-permute-start(f32[1,2,64]{2,1,0:T(2,128)} %get-tuple-element.48), channel_id=1, source_target_pairs={{16,0},{24,8},{32,16},{40,24},{48,32},{56,40},{64,48},{72,56},{80,... | collective-permute-start | bytes 1544 | tf_op jit(solution)/shard_map/ppermute | solution.py:12
  123.8 394.0 %collective-permute-start.6 = (f32[1,2,64]{2,1,0:T(2,128)}, f32[1,2,64]{2,1,0:T(2,128)}, u32[]{:S(2)}, u32[]{:S(2)}) collective-permute-start(f32[1,2,64]{2,1,0:T(2,128)} %get-tuple-element.52), channel_id=1, source_target_pairs={{760,0},{0,8},{8,16},{16,24},{24,32},{32,40},{40,48},{48,56},{56,6... | collective-permute-start | bytes 1544 | tf_op jit(solution)/shard_map/ppermute | solution.py:12
  464.6 32.9 %copy-start = (f32[10,3072]{1,0:T(8,128)S(1)}, f32[10,3072]{1,0:T(8,128)}, u32[]{:S(2)}) copy-start(f32[10,3072]{1,0:T(8,128)} %param.20) | copy-start | bytes 368644
  497.5 20.2 %copy-start.3 = (f32[1,2,64]{2,1,0:T(2,128)S(1)}, f32[1,2,64]{2,1,0:T(2,128)}, u32[]{:S(2)}) copy-start(f32[1,2,64]{2,1,0:T(2,128)} %get-tuple-element.51) | copy-start | bytes 1540
  497.6 27.8 %copy-start.2 = (f32[1,2,64]{2,1,0:T(2,128)S(1)}, f32[1,2,64]{2,1,0:T(2,128)}, u32[]{:S(2)}) copy-start(f32[1,2,64]{2,1,0:T(2,128)} %get-tuple-element.50) | copy-start | bytes 1540
  497.6 36.3 %copy-start.1 = (f32[1,2,64]{2,1,0:T(2,128)S(1)}, f32[1,2,64]{2,1,0:T(2,128)}, u32[]{:S(2)}) copy-start(f32[1,2,64]{2,1,0:T(2,128)} %get-tuple-element.49) | copy-start | bytes 1540
  517.7 7.6 %collective-permute-start.7 = (f32[1,2,64]{2,1,0:T(2,128)S(1)}, f32[1,2,64]{2,1,0:T(2,128)S(1)}, u32[]{:S(2)}, u32[]{:S(2)}) collective-permute-start(f32[1,2,64]{2,1,0:T(2,128)S(1)} %copy-done.3), channel_id=1, source_target_pairs={{752,0},{760,8},{0,16},{8,24},{16,32},{24,40},{32,48},{40,56},{48,... | collective-permute-start | bytes 1544 | tf_op jit(solution)/shard_map/ppermute | solution.py:12
  525.4 8.5 %collective-permute-start.8 = (f32[1,2,64]{2,1,0:T(2,128)S(1)}, f32[1,2,64]{2,1,0:T(2,128)S(1)}, u32[]{:S(2)}, u32[]{:S(2)}) collective-permute-start(f32[1,2,64]{2,1,0:T(2,128)S(1)} %copy-done.2), channel_id=1, source_target_pairs={{744,0},{752,8},{760,16},{0,24},{8,32},{16,40},{24,48},{32,56},{40... | collective-permute-start | bytes 1544 | tf_op jit(solution)/shard_map/ppermute | solution.py:12
  533.9 4.9 collective-permute-start.9
where the time goes:
time: 574 us; the launch traced here: 565 us
  local copies, waits for them, and re-layouts  413 us (72%)
  other arithmetic  68.5 us (12%)
  starting transfers between devices  58.2 us (10%)
  waiting for transfers between devices  24 us (4%)
    gather x6, local copies, waits for them, and re-layouts, lookup(): jnp.take(field, table.reshape(-1), axis=1)  382 us
    ppermute x12, starting transfers between devices, from_behind(): return lax.ppermute(block, axis, route)  51.6 us
    select_n x4, other arithmetic, lookup(): jnp.take(field, table.reshape(-1), axis=1)  33 us
    ppermute x12, waiting for transfers between devices, from_behind(): return lax.ppermute(block, axis, route)  24 us
    reduce_sum x1, other arithmetic, body(): tangent = jnp.sum(weights_on_edge * speed_near, axis=1)  17.2 us
  transfers between devices with their start and end apart: 14, of which 6 were waited for; matrix products, arithmetic and copies ran while one was open for 85% of the time, Pallas kernels for 0%

commit v1 on v0

v1 whole, which is shorter than its diff:
```python
import jax
import jax.numpy as jnp
from jax import lax
from jax.experimental import pallas as pl
from jax.experimental.pallas import tpu as pltpu
from jax.sharding import Mesh, PartitionSpec as P

OFF = (1, 2, 3, -1, -2, -3)
LANES = 128
ROWS = 24
LOCAL = ROWS * LANES
BLOCKS = 8

WAY = 6
RIM = 2 * WAY
TILES = RIM + 6
NEAR, MIDDLE, FAR, EDGE = 0, 12, 18, 22


def pick(table, low):
    return jnp.take_along_axis(table, low, axis=1, mode="promise_in_bounds")


def wide(row):
    return jnp.broadcast_to(row, (8, LANES))


def sublanes():
    return lax.broadcasted_iota(jnp.int32, (8, LANES), 0)


def total(tile):
    return jnp.sum(tile, axis=0, keepdims=True)


def halves(left, right):
    lane = lax.broadcasted_iota(jnp.int32, left.shape, 1)
    return jnp.where(lane < 64, left, right)


def turn(tile):
    return pltpu.roll(tile, 64, 1)


def pack_kernel(
    speed_hbm, height_hbm, vort_hbm, edge_list_hbm, cell_list_hbm, cells_hbm, share_hbm,
    sent_ref, table_ref,
    speed_ref, height_ref, vort_ref, edge_list_ref, cell_list_ref, cells_ref, share_ref, pair_ref, done,
):
    pairs = (
        (speed_hbm, speed_ref), (height_hbm, height_ref), (vort_hbm, vort_ref), (edge_list_hbm, edge_list_ref),
        (cell_list_hbm, cell_list_ref), (cells_hbm, cells_ref), (share_hbm, share_ref),
    )
    copies = [pltpu.make_async_copy(src, dst, done.at[i]) for i, (src, dst) in enumerate(pairs)]
    for copy in copies:
        copy.start()
    for copy in copies:
        copy.wait()
    for level in range(2):
        for row in range(ROWS):
            tile, place = level * 3 + row // 8, slice(row % 8, row % 8 + 1)
            columns = slice(row * LANES, (row + 1) * LANES)
            table_ref[tile, place, :] = speed_ref[level : level + 1, columns]
            table_ref[6 + tile, place, :] = height_ref[level : level + 1, columns]
            table_ref[12 + tile, place, :] = vort_ref[level : level + 1, columns]
    for tile in range(6):
        speed = table_ref[tile]
        mass = speed * table_ref[6 + tile]
        table_ref[6 + tile] = mass
        table_ref[12 + tile] = mass * table_ref[12 + tile]
        sent_ref[RIM + tile] = speed
    for way in range(2):
        for tile in (0, 1, 5):
            sent_ref[way * WAY + tile] = jnp.zeros((8, LANES), jnp.float32)
    spot = sublanes()
    for block in range(6):
        index = wide(edge_list_ref[block : block + 1, :])
        low, high = index & 127, index >> 7
        way, place = WAY * (block // 3), block % 3
        for field in range(6):
            found = jnp.zeros((8, LANES), jnp.float32)
            for part in range(3):
                got = pick(table_ref[field * 3 + part], low)
                found = jnp.where(high == spot + 8 * part, got, found)
            row, level = total(found), field % 2
            if field < 2:
                sent_ref[level, block : block + 1, :] = row
                sent_ref[WAY + level, block : block + 1, :] = row
            elif field < 4:
                sent_ref[way + 2 + place, 6 + level : 7 + level, :] = row
            else:
                sent_ref[way + 5, level * 3 + place : level * 3 + place + 1, :] = row
    pair_ref[...] = jnp.zeros((8, LANES), jnp.int32)
    for block in range(6):
        pair_ref[block : block + 1, 0:64] = cell_list_ref[block : block + 1, :]
    lists = pair_ref[...]
    turned = turn(lists)
    for group in range(3):
        index = wide(lists[2 * group : 2 * group + 1] + turned[2 * group + 1 : 2 * group + 2])
        low, high = index[:6] & 127, index[:6] >> 7
        edges = jnp.zeros((6, LANES), jnp.int32)
        shares = jnp.zeros((6, LANES), jnp.float32)
        for block in range(BLOCKS):
            columns = slice(block * LANES, (block + 1) * LANES)
            here = high == block
            edges = jnp.where(here, pick(cells_ref[:, columns], low), edges)
            shares = jnp.where(here, pick(share_ref[:, columns], low), shares)
        names = (edges - LOCAL).astype(jnp.float32)
        tables = (halves(names, turn(shares)), halves(turn(names), shares))
        sums = [jnp.zeros((8, LANES), jnp.float32) for _ in range(2)]
        for side in range(6):
            index, share = wide(edges[side : side + 1]), wide(shares[side : side + 1])
            low, high = index & 127, index >> 7
            for part in range(3):
                weight = jnp.where(high == spot + 8 * part, share, 0.0)
                for level in range(2):
                    got = pick(table_ref[level * 3 + part], low)
                    sums[level] = sums[level] + weight * (got * got)
        sums = [total(part) for part in sums]
        parts = (halves(sums[0], turn(sums[1])), halves(turn(sums[0]), sums[1]))
        for half in range(2):
            block = 2 * group + half
            way, place = WAY * (block // 3), block % 3
            sent_ref[way + 2 + place, 0:6, :] = tables[half]
            row = 6 + place % 2
            sent_ref[way + place // 2, row : row + 1, :] = parts[half]


def local_kernel(
    table_ref, near_ref, weight_ref, cells_ref, share_ref, sums_ref, energy_ref,
):
    spot = sublanes()
    table = table_ref[...].reshape(18 * 8, LANES)
    coarse = table.astype(jnp.bfloat16)
    fine = (table - coarse.astype(jnp.float32)).astype(jnp.bfloat16)
    table = jnp.concatenate([coarse, fine], axis=1)
    span = 2 * LANES
    counts = lax.broadcasted_iota(jnp.int32, (LANES, span), 0).astype(jnp.float32).astype(jnp.bfloat16)
    rows = lax.broadcasted_iota(jnp.int32, (8, span), 0)

    def edges(step, carry):
        columns = pl.ds(pl.multiple_of(step * span, span), span)
        sums = [jnp.zeros((8, span), jnp.float32) for _ in range(6)]
        for side in range(10):
            index = near_ref[side : side + 1, columns]
            weight = jnp.broadcast_to(weight_ref[side : side + 1, columns], (8, span))
            low = (index & 127).astype(jnp.float32).astype(jnp.bfloat16)
            high = jnp.broadcast_to(index >> 7, (8, span))
            ones = jnp.where(
                counts == jnp.broadcast_to(low, (LANES, span)), jnp.bfloat16(1), jnp.bfloat16(0)
            )
            got = jnp.dot(table, jnp.concatenate([ones, ones], axis=0), preferred_element_type=jnp.float32)
            for part in range(3):
                here = jnp.where(high == rows + 8 * part, weight, 0.0)
                for field in range(6):
                    row = (field * 3 + part) * 8
                    sums[field] = sums[field] + here * got[row : row + 8]
        for field in range(6):
            for half in range(2):
                sums_ref[step * 2 + half, field] = sums[field][:, half * LANES : (half + 1) * LANES]
        return carry

    lax.fori_loop(0, ROWS // 2, edges, 0, unroll=True)

    def cells(step, carry):
        columns = pl.ds(pl.multiple_of(step * LANES, LANES), LANES)
        sums = [jnp.zeros((8, LANES), jnp.float32) for _ in range(2)]
        for side in range(6):
            index = wide(cells_ref[side : side + 1, columns])
            share = wide(share_ref[side : side + 1, columns])
            low, high = index & 127, index >> 7
            for part in range(3):
                here = jnp.where(high == spot + 8 * part, share, 0.0)
                for level in range(2):
                    got = pick(table_ref[level * 3 + part], low)
                    sums[level] = sums[level] + here * (got * got)
        for level in range(2):
            energy_ref[step, level] = sums[level]
        return carry

    lax.fori_loop(0, BLOCKS, cells, 0, unroll=4)


def finish_kernel(
    core_ref, own_ref, around_ref, sums_ref, energy_sums_ref, near_ref, weight_ref, cells_ref, share_ref,
    ends_ref, inverse_ref, vort_ref, wind_ref, speed_ref, tendency_ref, tangent_ref, energy_ref,
    halo_ref, cell_ref,
):
    core = core_ref[0]
    first = jnp.full((8, LANES), core, jnp.int32) == 0
    spot = sublanes()

    def rows_at(way, tile, rows, place):
        chip, part = place // 2, place % 2
        side = 0 if chip < 0 else 1
        if chip == 0:
            return own_ref[part, way * WAY + tile, rows, :]
        if abs(chip) == 1:
            at = NEAR + part * WAY + tile
        elif abs(chip) == 2 and tile < 2:
            at = MIDDLE + part * 2 + tile
        elif abs(chip) == 2:
            assert part == 1 - side and tile >= 4
            at = MIDDLE + tile
        else:
            assert abs(chip) == 3 and tile < 2
            at = FAR + part * 2 + tile
        return around_ref[side, at, rows, :]

    def rows_of(distance, way, tile, start, stop):
        rows = slice(start, stop)
        on_first = rows_at(way, tile, rows, distance)
        on_second = rows_at(way, tile, rows, distance + 1)
        return jnp.where(first[: stop - start], on_first, on_second)

    for field in range(6):
        halo_ref[field] = jnp.zeros((8, LANES), jnp.float32)
    for block in range(6):
        away, way, place = -OFF[block], block // 3, block % 3
        mass = rows_of(away, way, 2 + place, 6, 8)
        for level in range(2):
            row = slice(block, block + 1)
            halo_ref[level, row, :] = rows_of(away, way, level, block, block + 1)
            halo_ref[2 + level, row, :] = mass[level : level + 1]
            at = level * 3 + place
            halo_ref[4 + level, row, :] = rows_of(away, way, 5, at, at + 1)

    squares = [halo_ref[level] * halo_ref[level] for level in range(2)]
    for step in range(BLOCKS):
        columns = slice(step * LANES, (step + 1) * LANES)
        sums = [energy_sums_ref[step, level] for level in range(2)]
        for side in range(6):
            index = wide(cells_ref[side : side + 1, columns])
            share = wide(share_ref[side : side + 1, columns])
            low, high = index & 127, index >> 7
            here = jnp.where(high == spot + ROWS, share, 0.0)
            for level in range(2):
                sums[level] = sums[level] + here * pick(squares[level], low)
        for level in range(2):
            row = total(sums[level])
            energy_ref[level : level + 1, columns] = row
            cell_ref[level, step : step + 1, :] = row

    for level in range(2):
        cell_ref[2 + level] = jnp.zeros((8, LANES), jnp.float32)
    for group in range(3):
        tables, names, parts = [], [], []
        for half in range(2):
            block = 2 * group + half
            away, way, place = -OFF[block], block // 3, block % 3
            for level in range(2):
                table = jnp.zeros((8, LANES), jnp.float32)
                for sender in range(6):
                    table = jnp.where(spot == sender, rows_of(away - OFF[sender], 0, level, 0, 8), table)
                tables.append(table * table)
            names.append(rows_of(away, way, 2 + place, 0, 8))
            row = 6 + place % 2
            parts.append(rows_of(away, way, place // 2, row, row + 1))
        indices = halves(names[0], turn(names[1])).astype(jnp.int32)
        shares = halves(turn(names[0]), names[1])
        parts = (halves(parts[0], turn(parts[1])), halves(turn(parts[0]), parts[1]))
        sums = [jnp.zeros((8, LANES), jnp.float32) for _ in range(2)]
        for side in range(6):
            index, share = wide(indices[side : side + 1]), wide(shares[side : side + 1])
            low, high = index & 127, index >> 7
            here = jnp.where(high == spot, share, 0.0)
            for level in range(2):
                got = halves(pick(tables[level], low), pick(tables[2 + level], low))
                sums[level] = sums[level] + here * got
        for level in range(2):
            cell_ref[2 + level, group : group + 1, :] = total(sums[level]) + parts[level]

    def edges(step, carry):
        columns = pl.ds(pl.multiple_of(step * LANES, LANES), LANES)
        sums = [sums_ref[step, field] for field in range(6)]
        for side in range(10):
            index = wide(near_ref[side : side + 1, columns])
            weight = wide(weight_ref[side : side + 1, columns])
            low, high = index & 127, index >> 7
            here = jnp.where(high == spot + ROWS, weight, 0.0)
            for field in range(6):
                sums[field] = sums[field] + here * pick(halo_ref[field], low)
        slopes = [jnp.zeros((8, LANES), jnp.float32) for _ in range(2)]
        for side in range(2):
            sign = 1.0 if side == 1 else -1.0
            index = wide(ends_ref[side : side + 1, columns])
            low, high = index & 127, index >> 7
            for part in range(2):
                here = high == spot + BLOCKS * part
                for level in range(2):
                    got = jnp.where(here, pick(cell_ref[2 * part + level], low), 0.0)
                    slopes[level] = slopes[level] + sign * got
        inverse = wide(inverse_ref[:, columns])
        row, tile = step % 8, step // 8
        below = around_ref[0, EDGE + core * 3 + tile, pl.ds(row, 1), :]
        above = around_ref[1, EDGE + core * 3 + tile, pl.ds(row, 1), :]
        speeds = [speed_ref[level : level + 1, columns] for level in range(2)]
        risers = [speeds[1] - below, above - speeds[0]]
        for level in range(2):
            vort = wide(vort_ref[level : level + 1, columns])
            flux = 0.5 * (vort * sums[2 + level] + sums[4 + level])
            result = total(flux - slopes[level] * inverse)
            advect = -0.5 * wind_ref[level : level + 1, columns] * risers[level]
            tendency_ref[level : level + 1, columns] = result + advect
            tangent_ref[level : level + 1, columns] = total(sums[level])
        return carry

    lax.fori_loop(0, ROWS, edges, 0, unroll=6)


VMEM = pl.BlockSpec(memory_space=pltpu.VMEM)


def body(
    velocity,
    thickness,
    vorticity,
    vertical_wind,
    weights_on_edge,
    edges_on_edge,
    edges_on_cell,
    cells_on_edge,
    energy_weight,
    inverse_distance,
    edge_halo_list,
    edge_halo_count,
    cell_halo_list,
    cell_halo_count,
):
    del edge_halo_count, cell_halo_count
    f32 = jnp.float32
    core = lax.axis_index("core")
    params = pltpu.CompilerParams(vmem_limit_bytes=24 << 20)
    inputs = (
        velocity, thickness, vorticity, edge_halo_list, cell_halo_list, edges_on_cell, energy_weight
    )
    sent, tables = pl.pallas_call(
        pack_kernel,
        out_shape=(
            jax.ShapeDtypeStruct((TILES, 8, LANES), f32),
            jax.ShapeDtypeStruct((18, 8, LANES), f32),
        ),
        in_specs=[pl.BlockSpec(memory_space=pltpu.HBM)] * 7,
        out_specs=(VMEM, VMEM),
        scratch_shapes=[pltpu.VMEM(x.shape, x.dtype) for x in inputs]
        + [pltpu.VMEM((8, LANES), jnp.int32), pltpu.SemaphoreType.DMA((7,))],
        compiler_params=pltpu.CompilerParams(vmem_limit_bytes=60 << 20),
        name="pack",
    )(*inputs)

    mesh_axes = ("x", "z", "core")
    own = lax.all_gather(sent, "core")
    even = core == 0
    near = jnp.where(even, own[:, :WAY], own[:, WAY:RIM])
    rims = jnp.where(even, own[:, RIM + 3 :], own[:, RIM : RIM + 3])
    chips = lax.axis_size("x") * lax.axis_size("z")

    def apart(block, distance):
        right = [(2 * c, 2 * ((c + distance) % chips)) for c in range(chips)]
        left = [(2 * c + 1, 2 * ((c - distance) % chips) + 1) for c in range(chips)]
        return lax.ppermute(block, mesh_axes, right + left)

    groups = lax.axis_size("lev")
    up = [(i, i + 1) for i in range(groups - 1)]
    down = [(groups + i + 1, groups + i) for i in range(groups - 1)]
    speeds = near[:, :2].reshape(4, 8, LANES)
    rest = jnp.where(even, near[1, 4:], near[0, 4:])
    arrived = [
        apart(near, 1).reshape(12, 8, LANES),
        apart(jnp.concatenate([speeds, rest], axis=0), 2),
        apart(speeds, 3),
        lax.ppermute(rims, ("core", "lev"), up + down).reshape(6, 8, LANES),
    ]
    arrived = jnp.concatenate(arrived, axis=0)
    sums, energy_sums = pl.pallas_call(
        local_kernel,
        out_shape=(
            jax.ShapeDtypeStruct((ROWS, 6, 8, LANES), f32),
            jax.ShapeDtypeStruct((BLOCKS, 2, 8, LANES), f32),
        ),
        in_specs=[VMEM] * 5,
        out_specs=(VMEM, VMEM),
        compiler_params=params,
        cost_estimate=pl.CostEstimate(flops=20_000_000, bytes_accessed=1_000_000, transcendentals=0),
        name="local",
    )(tables, edges_on_edge, weights_on_edge, edges_on_cell, energy_weight)
    around = lax.all_gather(arrived, "core")
    return pl.pallas_call(
        finish_kernel,
        out_shape=(
            jax.ShapeDtypeStruct(velocity.shape, f32),
            jax.ShapeDtypeStruct(velocity.shape, f32),
            jax.ShapeDtypeStruct((velocity.shape[0], edges_on_cell.shape[1]), f32),
        ),
        in_specs=[pl.BlockSpec(memory_space=pltpu.SMEM)] + [VMEM] * 13,
        out_specs=(VMEM, VMEM, VMEM),
        scratch_shapes=[pltpu.VMEM((6, 8, LANES), f32), pltpu.VMEM((4, 8, LANES), f32)],
        compiler_params=params,
        name="finish",
    )(
        core.astype(jnp.int32).reshape(1), own, around, sums, energy_sums, edges_on_edge, weights_on_edge,
        edges_on_cell, energy_weight, cells_on_edge, inverse_distance.reshape(1, -1), vorticity,
        vertical_wind, velocity,
    )


def solution(mesh):
    fine = Mesh(mesh.devices.reshape(4, 12, 2, 8), ("x", "z", "core", "lev"))
    parts = ("x", "z", "core")
    in_specs = (
        P("lev", parts),
        P("lev", parts),
        P("lev", parts),
        P("lev", parts),
        P(None, parts),
        P(None, parts),
        P(None, parts),
        P(None, parts),
        P(None, parts),
        P(parts),
        P(parts, None),
        P(parts),
        P(parts, None),
        P(parts),
    )
    out_specs = (P("lev", parts), P("lev", parts), P("lev", parts))
    return jax.shard_map(body, mesh=fine, in_specs=in_specs, out_specs=out_specs, check_vma=False)
```

time: 574 us -> 42.1 us (0.07)
  the two profiles are of different devices: /device:TPU:1 before, /device:TPU:25 now
where the time goes in v1:
time: 42.1 us; the launch traced here: 41.7 us
  starting transfers between devices  24 us (57%)
  Pallas kernels  9.7 us (23%)
  blocking collectives  7 us (17%)
  between operations  0.88 us (2%)
    ppermute x3, starting transfers between devices, apart(): return lax.ppermute(block, mesh_axes, right + left)  21.8 us
    all_gather x1, blocking collectives, body(): around = lax.all_gather(arrived, 'core')  4.42 us
    pallas_call x1, Pallas kernels, body(): pl.pallas_call(finish_kernel, out_shape=(jax.ShapeDtypeStruct(velocity.sh...  4.25 us
    pallas_call x1, Pallas kernels, body(): pl.pallas_call(local_kernel, out_shape=(jax.ShapeDtypeStruct((ROWS, 6, 8,...  3.11 us
    all_gather x1, blocking collectives, body(): own = lax.all_gather(sent, 'core')  2.58 us
    pallas_call x1, Pallas kernels, body(): pl.pallas_call(pack_kernel, out_shape=(jax.ShapeDtypeStruct((TILES, 8, LA...  2.34 us
    ppermute x1, starting transfers between devices, body(): lax.ppermute(rims, ('core', 'lev'), up + down).reshape(6, 8, LANES)  2.2 us
  transfers between devices with their start and end apart: 4, of which 0 were waited for; matrix products, arithmetic and copies ran while one was open for 0% of the time, Pallas kernels for 7%

profile of v1, /device:TPU:25, one launch (start us, length us, event | category | flops | bytes accessed | tf_op | source)
XLA Modules:
  0.0 41.7 jit_solution(8886226153624524668)
XLA Ops:
  0.6 2.3 %pack.1 = (f32[18,8,128]{2,1,0:T(8,128)}, f32[18,8,128]{2,1,0:T(8,128)}) custom-call(f32[2,3072]{1,0:T(2,128)} %speed_ref.1, f32[2,3072]{1,0:T(2,128)} %height_hbm.1, f32[2,3072]{1,0:T(2,128)} %vort_ref.1, s32[6,128]{1,0:T(8,128)} %edge_list_hbm.1, s32[6,64]{1,0:T(8,128)} %cell_list_hbm.1, s32[6,1024]{1,0:T(8,128)} %cells_ref.3, f32[6,1024]{1,0:T(8,128)} %share_ref.3), custom_call_target="tpu_custom_call" | custom-call | tf_op jit(solution)/shard_map/pack/pallas_call | solution.py:337
  3.0 0.0 copy-start.1
  3.0 2.6 %all-gather = f32[36,8,128]{2,1,0:T(8,128)S(1)} all-gather(f32[18,8,128]{2,1,0:T(8,128)} %get-tuple-element.7), channel_id=2, replica_groups=mesh['x'=4,'z'=12,'core'=2,'lev'=8] {'core'}, dimensions={0}, use_global_device_ids=true | all-gather | bytes 221184 | tf_op jit(solution)/shard_map/all_gather | solution.py:352
  5.6 0.0 copy-start
  5.6 2.2 %collective-permute-start.3 = (f32[2,3,8,128]{3,2,1,0:T(8,128)S(1)}, f32[2,3,8,128]{3,2,1,0:T(8,128)S(1)}, u32[]{:S(2)}, u32[]{:S(2)}) collective-permute-start(f32[2,3,8,128]{3,2,1,0:T(8,128)S(1)} %slice_select_fusion.1), channel_id=1, source_target_pairs={{0,1},{1,2},{2,3},{3,4},{4,5},{5,6},{6,7},{9,8},{10,9},{11,10},{12... | collective-permute-start | bytes 73736 | tf_op jit(solution)/shard_map/ppermute | solution.py:372
  7.8 0.0 copy-start.6
  7.8 16.5 %collective-permute-start = (f32[2,6,8,128]{3,2,1,0:T(8,128)S(1)}, f32[2,6,8,128]{3,2,1,0:T(8,128)S(1)}, u32[]{:S(2)}, u32[]{:S(2)}) collective-permute-start(f32[2,6,8,128]{3,2,1,0:T(8,128)S(1)} %slice_select_fusion), channel_id=1, source_target_pairs={{0,16},{16,32},{32,48},{48,64},{64,80},{80,96},{96,112},{112,128},... | collective-permute-start | bytes 147464 | tf_op jit(solution)/shard_map/ppermute | solution.py:361
  24.3 0.0 copy-start.3
  24.4 0.0 copy-start.2
  24.4 2.2 %collective-permute-start.1 = (f32[6,8,128]{2,1,0:T(8,128)S(1)}, f32[6,8,128]{2,1,0:T(8,128)S(1)}, u32[]{:S(2)}, u32[]{:S(2)}) collective-permute-start(f32[6,8,128]{2,1,0:T(8,128)S(1)} %pad_maximum_fusion.1), channel_id=1, source_target_pairs={{0,32},{16,48},{32,64},{48,80},{64,96},{80,112},{96,128},{112,144}... | collective-permute-start | bytes 73736 | tf_op jit(solution)/shard_map/ppermute | solution.py:361
  26.6 3.1 %collective-permute-start.2 = (f32[4,8,128]{2,1,0:T(8,128)S(1)}, f32[4,8,128]{2,1,0:T(8,128)S(1)}, u32[]{:S(2)}, u32[]{:S(2)}) collective-permute-start(f32[4,8,128]{2,1,0:T(8,128)S(1)} %bitcast.15), channel_id=1, source_target_pairs={{0,48},{16,64},{32,80},{48,96},{64,112},{80,128},{96,144},{112,160... | collective-permute-start | bytes 49160 | tf_op jit(solution)/shard_map/ppermute | solution.py:361
  29.7 0.0 copy-done.1
  29.7 0.0 copy-done
  29.7 0.0 copy-done.6
  29.7 0.0 copy-done.3
  29.7 0.0 copy-done.2
  29.7 3.1 %local.1 = (f32[24,6,8,128]{3,2,1,0:T(8,128)S(1)}, f32[8,2,8,128]{3,2,1,0:T(8,128)S(1)}) custom-call(f32[18,8,128]{2,1,0:T(8,128)S(1)} %copy-done.6, s32[10,3072]{1,0:T(8,128)S(1)} %copy-done, f32[10,3072]{1,0:T(8,128)S(1)} %copy-done.1, s32[6,1024]{1,0:T(8,128)S(1)} %copy-done.2, f32[6,1024]{1,0:T(8,128)S(1)} %copy-done.3), custom_call_target="tpu_custom_call" | custom-call | flops 20000000 | bytes 1000000 | tf_op jit(solution)/shard_map/local/pallas_call | solution.py:375
  32.8 0.0 collective-permute-done.2
  32.9 0.0 collective-permute-done.3
  32.9 0.0 collective-permute-done.1
  32.9 0.0 collective-permute-done
  32.9 0.0 copy-start.4
  32.9 0.0 copy-start.5
  32.9 0.0 copy-start.7
  32.9 0.0 copy-start.8
  33.0 0.0 copy-start.9
  33.0 4.4 %all-gather.1 = f32[56,8,128]{2,1,0:T(8,128)S(1)} all-gather(f32[28,8,128]{2,1,0:T(8,128)S(1)} %pad_maximum_fusion), channel_id=3, replica_groups=mesh['x'=4,'z'=12,'core'=2,'lev'=8] {'core'}, dimensions={0}, use_global_device_ids=true | all-gather | bytes 344064 | tf_op jit(solution)/shard_map/all_gather | solution.py:387
  37.4 0.0 copy-done.4
  37.4 0.0 copy-done.5
  37.4 0.0 copy-done.7
  37.4 0.0 copy-done.8
  37.4 0.0 copy-done.9
  37.4 4.3 %finish.1 = (f32[2,3072]{1,0:T(2,128)}, f32[2,3072]{1,0:T(2,128)}, f32[2,1024]{1,0:T(2,128)}) custom-call(s32[1]{0:T(128)} %bitcast.core_ref, f32[2,18,8,128]{3,2,1,0:T(8,128)S(1)} %bitcast.11, f32[2,28,8,128]{3,2,1,0:T(8,128)S(1)} %bitcast.12, f32[24,6,8,128]{3,2,1,0:T(8,128)S(1)} %get-tuple-element.9.sums_ref, ...), custom_call_target="tpu_custom_call" | custom-call | tf_op jit(solution)/shard_map/finish/pallas_call | solution.py:388
  (6 shorter events, 0.0 us)
Async XLA Ops:
  3.0 26.7 %copy-start.1 = (f32[10,3072]{1,0:T(8,128)S(1)}, f32[10,3072]{1,0:T(8,128)}, u32[]{:S(2)}) copy-start(f32[10,3072]{1,0:T(8,128)} %weight_ref.3) | copy-start | bytes 368644
  5.6 24.1 %copy-start = (s32[10,3072]{1,0:T(8,128)S(1)}, s32[10,3072]{1,0:T(8,128)}, u32[]{:S(2)}) copy-start(s32[10,3072]{1,0:T(8,128)} %near_ref.3) | copy-start | bytes 368644
  5.6 27.3 %collective-permute-start.3 = (f32[2,3,8,128]{3,2,1,0:T(8,128)S(1)}, f32[2,3,8,128]{3,2,1,0:T(8,128)S(1)}, u32[]{:S(2)}, u32[]{:S(2)}) collective-permute-start(f32[2,3,8,128]{3,2,1,0:T(8,128)S(1)} %slice_select_fusion.1), channel_id=1, source_target_pairs={{0,1},{1,2},{2,3},{3,4},{4,5},{5,6},{6,7},{9,8},{10,9},{11,10},{12... | collective-permute-start | bytes 73736 | tf_op jit(solution)/shard_map/ppermute | solution.py:372
  7.8 21.9 %copy-start.6 = (f32[18,8,128]{2,1,0:T(8,128)S(1)}, f32[18,8,128]{2,1,0:T(8,128)}, u32[]{:S(2)}) copy-start(f32[18,8,128]{2,1,0:T(8,128)} %get-tuple-element.8.table_ref) | copy-start | bytes 221188
  7.8 25.1 %collective-permute-start = (f32[2,6,8,128]{3,2,1,0:T(8,128)S(1)}, f32[2,6,8,128]{3,2,1,0:T(8,128)S(1)}, u32[]{:S(2)}, u32[]{:S(2)}) collective-permute-start(f32[2,6,8,128]{3,2,1,0:T(8,128)S(1)} %slice_select_fusion), channel_id=1, source_target_pairs={{0,16},{16,32},{32,48},{48,64},{64,80},{80,96},{96,112},{112,128},... | collective-permute-start | bytes 147464 | tf_op jit(solution)/shard_map/ppermute | solution.py:361
  24.3 5.4 %copy-start.3 = (f32[6,1024]{1,0:T(8,128)S(1)}, f32[6,1024]{1,0:T(8,128)}, u32[]{:S(2)}) copy-start(f32[6,1024]{1,0:T(8,128)} %share_ref.3) | copy-start | bytes 73732
  24.4 5.4 %copy-start.2 = (s32[6,1024]{1,0:T(8,128)S(1)}, s32[6,1024]{1,0:T(8,128)}, u32[]{:S(2)}) copy-start(s32[6,1024]{1,0:T(8,128)} %cells_ref.3) | copy-start | bytes 73732
  24.4 8.5 %collective-permute-start.1 = (f32[6,8,128]{2,1,0:T(8,128)S(1)}, f32[6,8,128]{2,1,0:T(8,128)S(1)}, u32[]{:S(2)}, u32[]{:S(2)}) collective-permute-start(f32[6,8,128]{2,1,0:T(8,128)S(1)} %pad_maximum_fusion.1), channel_id=1, source_target_pairs={{0,32},{16,48},{32,64},{48,80},{64,96},{80,112},{96,128},{112,144}... | collective-permute-start | bytes 73736 | tf_op jit(solution)/shard_map/ppermute | solution.py:361
  26.6 6.3 %collective-permute-start.2 = (f32[4,8,128]{2,1,0:T(8,128)S(1)}, f32[4,8,128]{2,1,0:T(8,128)S(1)}, u32[]{:S(2)}, u32[]{:S(2)}) collective-permute-start(f32[4,8,128]{2,1,0:T(8,128)S(1)} %bitcast.15), channel_id=1, source_target_pairs={{0,48},{16,64},{32,80},{48,96},{64,112},{80,128},{96,144},{112,160... | collective-permute-start | bytes 49160 | tf_op jit(solution)/shard_map/ppermute | solution.py:361
  32.9 4.5 %copy-start.4 = (f32[2,3072]{1,0:T(2,128)S(1)}, f32[2,3072]{1,0:T(2,128)}, u32[]{:S(2)}) copy-start(f32[2,3072]{1,0:T(2,128)} %speed_ref.1) | copy-start | bytes 73732
  32.9 4.5 %copy-start.5 = (f32[2,3072]{1,0:T(2,128)S(1)}, f32[2,3072]{1,0:T(2,128)}, u32[]{:S(2)}) copy-start(f32[2,3072]{1,0:T(2,128)} %vort_ref.1) | copy-start | bytes 73732
  32.9 4.5 %copy-start.7 = (s32[2,3072]{1,0:T(2,128)S(1)}, s32[2,3072]{1,0:T(2,128)}, u32[]{:S(2)}) copy-start(s32[2,3072]{1,0:T(2,128)} %ends_ref.1) | copy-start | bytes 73732
  32.9 4.5 %copy-start.8 = (f32[2,3072]{1,0:T(2,128)S(1)}, f32[2,3072]{1,0:T(2,128)}, u32[]{:S(2)}) copy-start(f32[2,3072]{1,0:T(2,128)} %wind_ref.1) | copy-start | bytes 73732
  33.0 4.5 %copy-start.9 = (f32[3072]{0:T(1024)S(1)}, f32[3072]{0:T(1024)}, u32[]{:S(2)}) copy-start(f32[3072]{0:T(1024)} %param.23) | copy-start | bytes 36868

commit v2 on v1

--- a/solution.py
+++ b/solution.py
@@ -14,7 +14,7 @@
 WAY = 6
 RIM = 2 * WAY
 TILES = RIM + 6
-NEAR, MIDDLE, FAR, EDGE = 0, 12, 18, 22
+NEAR, MIDDLE, FAR, EDGE = 0, 12, 19, 27
 
 
 def pick(table, low):
@@ -31,6 +31,30 @@
 
 def total(tile):
     return jnp.sum(tile, axis=0, keepdims=True)
+
+
+SPAN = 2 * LANES
+PRODUCTS = 9
+
+
+def split(table, axis):
+    coarse = table.astype(jnp.bfloat16)
+    fine = (table - coarse.astype(jnp.float32)).astype(jnp.bfloat16)
+    return jnp.concatenate([coarse, fine], axis=axis)
+
+
+def ones_at(index, counts):
+    low = (index & 127).astype(jnp.float32).astype(jnp.bfloat16)
+    here = counts == jnp.broadcast_to(low, (LANES, SPAN))
+    return jnp.where(here, jnp.bfloat16(1), jnp.bfloat16(0))
+
+
+def product(table, ones):
+    return jnp.dot(table, ones, preferred_element_type=jnp.float32)
+
+
+def counting():
+    return lax.broadcasted_iota(jnp.int32, (LANES, SPAN), 0).astype(jnp.float32).astype(jnp.bfloat16)
 
 
 def halves(left, right):
@@ -130,34 +154,33 @@
     table_ref, near_ref, weight_ref, cells_ref, share_ref, sums_ref, energy_ref,
 ):
     spot = sublanes()
-    table = table_ref[...].reshape(18 * 8, LANES)
-    coarse = table.astype(jnp.bfloat16)
-    fine = (table - coarse.astype(jnp.float32)).astype(jnp.bfloat16)
-    table = jnp.concatenate([coarse, fine], axis=1)
-    span = 2 * LANES
-    counts = lax.broadcasted_iota(jnp.int32, (LANES, span), 0).astype(jnp.float32).astype(jnp.bfloat16)
-    rows = lax.broadcasted_iota(jnp.int32, (8, span), 0)
+    table = split(table_ref[...].reshape(18 * 8, LANES), 1)
+    counts = counting()
 
     def edges(step, carry):
-        columns = pl.ds(pl.multiple_of(step * span, span), span)
-        sums = [jnp.zeros((8, span), jnp.float32) for _ in range(6)]
+        columns = pl.ds(pl.multiple_of(step * SPAN, SPAN), SPAN)
+        sums = [[jnp.zeros((8, LANES), jnp.float32) for _ in range(6)] for _ in range(2)]
         for side in range(10):
-            index = near_ref[side : side + 1, columns]
-            weight = jnp.broadcast_to(weight_ref[side : side + 1, columns], (8, span))
-            low = (index & 127).astype(jnp.float32).astype(jnp.bfloat16)
-            high = jnp.broadcast_to(index >> 7, (8, span))
-            ones = jnp.where(
-                counts == jnp.broadcast_to(low, (LANES, span)), jnp.bfloat16(1), jnp.bfloat16(0)
-            )
-            got = jnp.dot(table, jnp.concatenate([ones, ones], axis=0), preferred_element_type=jnp.float32)
-            for part in range(3):
-                here = jnp.where(high == rows + 8 * part, weight, 0.0)
-                for field in range(6):
-                    row = (field * 3 + part) * 8
-                    sums[field] = sums[field] + here * got[row : row + 8]
-        for field in range(6):
+            index, weight = near_ref[side : side + 1, columns], weight_ref[side : side + 1, columns]
+            if side < PRODUCTS:
+                ones = ones_at(index, counts)
+                got = product(table, jnp.concatenate([ones, ones], axis=0))
             for half in range(2):
-                sums_ref[step * 2 + half, field] = sums[field][:, half * LANES : (half + 1) * LANES]
+                part_of = slice(half * LANES, (half + 1) * LANES)
+                low, high = wide(index[:, part_of]) & 127, wide(index[:, part_of]) >> 7
+                share = wide(weight[:, part_of])
+                for part in range(3):
+                    here = jnp.where(high == spot + 8 * part, share, 0.0)
+                    for field in range(6):
+                        tile = field * 3 + part
+                        if side < PRODUCTS:
+                            values = got[tile * 8 : tile * 8 + 8, part_of]
+                        else:
+                            values = pick(table_ref[tile], low)
+                        sums[half][field] = sums[half][field] + here * values
+        for half in range(2):
+            for field in range(6):
+                sums_ref[step * 2 + half, field] = sums[half][field]
         return carry
 
     lax.fori_loop(0, ROWS // 2, edges, 0, unroll=True)
@@ -270,42 +293,52 @@
         for level in range(2):
             cell_ref[2 + level, group : group + 1, :] = total(sums[level]) + parts[level]
 
+    halo = split(halo_ref[...].reshape(6 * 8, LANES), 0)
+    counts = counting()
+
     def edges(step, carry):
-        columns = pl.ds(pl.multiple_of(step * LANES, LANES), LANES)
-        sums = [sums_ref[step, field] for field in range(6)]
+        columns = pl.ds(pl.multiple_of(step * SPAN, SPAN), SPAN)
+        sums = [[sums_ref[step * 2 + half, field] for field in range(6)] for half in range(2)]
         for side in range(10):
-            index = wide(near_ref[side : side + 1, columns])
-            weight = wide(weight_ref[side : side + 1, columns])
-            low, high = index & 127, index >> 7
-            here = jnp.where(high == spot + ROWS, weight, 0.0)
-            for field in range(6):
-                sums[field] = sums[field] + here * pick(halo_ref[field], low)
-        slopes = [jnp.zeros((8, LANES), jnp.float32) for _ in range(2)]
-        for side in range(2):
-            sign = 1.0 if side == 1 else -1.0
-            index = wide(ends_ref[side : side + 1, columns])
-            low, high = index & 127, index >> 7
-            for part in range(2):
-                here = high == spot + BLOCKS * part
-                for level in range(2):
-                    got = jnp.where(here, pick(cell_ref[2 * part + level], low), 0.0)
-                    slopes[level] = slopes[level] + sign * got
-        inverse = wide(inverse_ref[:, columns])
-        row, tile = step % 8, step // 8
-        below = around_ref[0, EDGE + core * 3 + tile, pl.ds(row, 1), :]
-        above = around_ref[1, EDGE + core * 3 + tile, pl.ds(row, 1), :]
-        speeds = [speed_ref[level : level + 1, columns] for level in range(2)]
-        risers = [speeds[1] - below, above - speeds[0]]
-        for level in range(2):
-            vort = wide(vort_ref[level : level + 1, columns])
-            flux = 0.5 * (vort * sums[2 + level] + sums[4 + level])
-            result = total(flux - slopes[level] * inverse)
-            advect = -0.5 * wind_ref[level : level + 1, columns] * risers[level]
-            tendency_ref[level : level + 1, columns] = result + advect
-            tangent_ref[level : level + 1, columns] = total(sums[level])
+            index, weight = near_ref[side : side + 1, columns], weight_ref[side : side + 1, columns]
+            got = product(halo, ones_at(index, counts))
+            got = got[:48] + got[48:]
+            for half in range(2):
+                part_of = slice(half * LANES, (half + 1) * LANES)
+                high = wide(index[:, part_of]) >> 7
+                here = jnp.where(high == spot + ROWS, wide(weight[:, part_of]), 0.0)
+                for field in range(6):
+                    values = got[field * 8 : field * 8 + 8, part_of]
+                    sums[half][field] = sums[half][field] + here * values
+        for half in range(2):
+            block = step * 2 + half
+            columns = pl.ds(pl.multiple_of(block * LANES, LANES), LANES)
+            slopes = [jnp.zeros((8, LANES), jnp.float32) for _ in range(2)]
+            for side in range(2):
+                sign = 1.0 if side == 1 else -1.0
+                index = wide(ends_ref[side : side + 1, columns])
+                low, high = index & 127, index >> 7
+                for part in range(2):
+                    here = high == spot + BLOCKS * part
+                    for level in range(2):
+                        got = jnp.where(here, pick(cell_ref[2 * part + level], low), 0.0)
+                        slopes[level] = slopes[level] + sign * got
+            inverse = wide(inverse_ref[:, columns])
+            row, tile = block % 8, block // 8
+            below = around_ref[0, EDGE + core * 3 + tile, pl.ds(row, 1), :]
+            above = around_ref[1, EDGE + core * 3 + tile, pl.ds(row, 1), :]
+            speeds = [speed_ref[level : level + 1, columns] for level in range(2)]
+            risers = [speeds[1] - below, above - speeds[0]]
+            for level in range(2):
+                vort = wide(vort_ref[level : level + 1, columns])
+                flux = 0.5 * (vort * sums[half][2 + level] + sums[half][4 + level])
+                result = total(flux - slopes[level] * inverse)
+                advect = -0.5 * wind_ref[level : level + 1, columns] * risers[level]
+                tendency_ref[level : level + 1, columns] = result + advect
+                tangent_ref[level : level + 1, columns] = total(sums[half][level])
         return carry
 
-    lax.fori_loop(0, ROWS, edges, 0, unroll=6)
+    lax.fori_loop(0, ROWS // 2, edges, 0, unroll=True)
 
 
 VMEM = pl.BlockSpec(memory_space=pltpu.VMEM)
@@ -365,10 +398,11 @@
     down = [(groups + i + 1, groups + i) for i in range(groups - 1)]
     speeds = near[:, :2].reshape(4, 8, LANES)
     rest = jnp.where(even, near[1, 4:], near[0, 4:])
+    spare = near[1]
     arrived = [
         apart(near, 1).reshape(12, 8, LANES),
-        apart(jnp.concatenate([speeds, rest], axis=0), 2),
-        apart(speeds, 3),
+        apart(jnp.concatenate([speeds, rest, spare[:1]], axis=0), 2),
+        apart(jnp.concatenate([speeds, spare[:4]], axis=0), 3),
         lax.ppermute(rims, ("core", "lev"), up + down).reshape(6, 8, LANES),
     ]
     arrived = jnp.concatenate(arrived, axis=0)

time: 42.1 us -> 39 us (0.926)
  the two profiles are of different devices: /device:TPU:25 before, /device:TPU:57 now
where the time goes in v2:
time: 39 us; the launch traced here: 38.5 us
  starting transfers between devices  24.9 us (64%)
  Pallas kernels  7.93 us (20%)
  blocking collectives  4.71 us (12%)
  between operations  0.9 us (2%)
    ppermute x3, starting transfers between devices, apart(): return lax.ppermute(block, mesh_axes, right + left)  21.9 us
    pallas_call x1, Pallas kernels, body(): pl.pallas_call(local_kernel, out_shape=(jax.ShapeDtypeStruct((ROWS, 6, 8,...  3.02 us
    ppermute x1, starting transfers between devices, body(): lax.ppermute(rims, ('core', 'lev'), up + down).reshape(6, 8, LANES)  2.97 us
    all_gather x1, blocking collectives, body(): own = lax.all_gather(sent, 'core')  2.58 us
    pallas_call x1, Pallas kernels, body(): pl.pallas_call(finish_kernel, out_shape=(jax.ShapeDtypeStruct(velocity.sh...  2.57 us
    pallas_call x1, Pallas kernels, body(): pl.pallas_call(pack_kernel, out_shape=(jax.ShapeDtypeStruct((TILES, 8, LA...  2.34 us
    all_gather x1, blocking collectives, body(): around = lax.all_gather(arrived, 'core')  2.13 us
  transfers between devices with their start and end apart: 4, of which 0 were waited for; matrix products, arithmetic and copies ran while one was open for 0% of the time, Pallas kernels for 8%

profile of v2, /device:TPU:57, one launch (start us, length us, event | category | flops | bytes accessed | tf_op | source)
XLA Modules:
  0.0 38.5 jit_solution(930928026612431495)
XLA Ops:
  0.6 2.3 %pack.1 = (f32[18,8,128]{2,1,0:T(8,128)}, f32[18,8,128]{2,1,0:T(8,128)}) custom-call(f32[2,3072]{1,0:T(2,128)} %speed_ref.1, f32[2,3072]{1,0:T(2,128)} %height_hbm.1, f32[2,3072]{1,0:T(2,128)} %vort_ref.1, s32[6,128]{1,0:T(8,128)} %edge_list_hbm.1, s32[6,64]{1,0:T(8,128)} %cell_list_hbm.1, s32[6,1024]{1,0:T(8,128)} %cells_ref.3, f32[6,1024]{1,0:T(8,128)} %share_ref.3), custom_call_target="tpu_custom_call" | custom-call | tf_op jit(solution)/shard_map/pack/pallas_call | solution.py:370
  3.0 0.0 copy-start.3
  3.0 0.0 copy-start.6
  3.0 2.6 %all-gather = f32[36,8,128]{2,1,0:T(8,128)S(1)} all-gather(f32[18,8,128]{2,1,0:T(8,128)} %get-tuple-element.7), channel_id=2, replica_groups=mesh['x'=4,'z'=12,'core'=2,'lev'=8] {'core'}, dimensions={0}, use_global_device_ids=true | all-gather | bytes 221184 | tf_op jit(solution)/shard_map/all_gather | solution.py:385
  5.6 0.0 copy-start
  5.6 0.0 copy-start.1
  5.6 16.6 %collective-permute-start = (f32[2,6,8,128]{3,2,1,0:T(8,128)S(1)}, f32[2,6,8,128]{3,2,1,0:T(8,128)S(1)}, u32[]{:S(2)}, u32[]{:S(2)}) collective-permute-start(f32[2,6,8,128]{3,2,1,0:T(8,128)S(1)} %slice_select_fusion), channel_id=1, source_target_pairs={{0,16},{16,32},{32,48},{48,64},{64,80},{80,96},{96,112},{112,128},... | collective-permute-start | bytes 147464 | tf_op jit(solution)/shard_map/ppermute | solution.py:394
  22.3 2.2 %collective-permute-start.1 = (f32[7,8,128]{2,1,0:T(8,128)S(1)}, f32[7,8,128]{2,1,0:T(8,128)S(1)}, u32[]{:S(2)}, u32[]{:S(2)}) collective-permute-start(f32[7,8,128]{2,1,0:T(8,128)S(1)} %pad_maximum_fusion.2), channel_id=1, source_target_pairs={{0,32},{16,48},{32,64},{48,80},{64,96},{80,112},{96,128},{112,144}... | collective-permute-start | bytes 86024 | tf_op jit(solution)/shard_map/ppermute | solution.py:394
  24.5 0.0 copy-start.2
  24.5 3.1 %collective-permute-start.2 = (f32[8,8,128]{2,1,0:T(8,128)S(1)}, f32[8,8,128]{2,1,0:T(8,128)S(1)}, u32[]{:S(2)}, u32[]{:S(2)}) collective-permute-start(f32[8,8,128]{2,1,0:T(8,128)S(1)} %pad_maximum_fusion.1), channel_id=1, source_target_pairs={{0,48},{16,64},{32,80},{48,96},{64,112},{80,128},{96,144},{112,160... | collective-permute-start | bytes 98312 | tf_op jit(solution)/shard_map/ppermute | solution.py:394
  27.6 3.0 %collective-permute-start.3 = (f32[2,3,8,128]{3,2,1,0:T(8,128)S(1)}, f32[2,3,8,128]{3,2,1,0:T(8,128)S(1)}, u32[]{:S(2)}, u32[]{:S(2)}) collective-permute-start(f32[2,3,8,128]{3,2,1,0:T(8,128)S(1)} %slice_select_fusion.1), channel_id=1, source_target_pairs={{0,1},{1,2},{2,3},{3,4},{4,5},{5,6},{6,7},{9,8},{10,9},{11,10},{12... | collective-permute-start | bytes 73736 | tf_op jit(solution)/shard_map/ppermute | solution.py:406
  30.6 0.0 copy-done.3
  30.6 0.0 copy-done.6
  30.6 0.0 copy-done
  30.6 0.0 copy-done.1
  30.7 0.0 copy-done.2
  30.7 3.0 %local.1 = (f32[24,6,8,128]{3,2,1,0:T(8,128)S(1)}, f32[8,2,8,128]{3,2,1,0:T(8,128)S(1)}) custom-call(f32[18,8,128]{2,1,0:T(8,128)S(1)} %copy-done.6, s32[10,3072]{1,0:T(8,128)S(1)} %copy-done, f32[10,3072]{1,0:T(8,128)S(1)} %copy-done.1, s32[6,1024]{1,0:T(8,128)S(1)} %copy-done.2, f32[6,1024]{1,0:T(8,128)S(1)} %copy-done.3), custom_call_target="tpu_custom_call" | custom-call | flops 20000000 | bytes 1000000 | tf_op jit(solution)/shard_map/local/pallas_call | solution.py:409
  33.7 0.0 collective-permute-done.3
  33.7 0.0 collective-permute-done.1
  33.7 0.0 collective-permute-done.2
  33.7 0.0 collective-permute-done
  33.7 0.0 copy-start.4
  33.8 0.0 copy-start.5
  33.8 0.0 copy-start.7
  33.8 0.0 copy-start.8
  33.8 0.0 copy-start.9
  33.8 2.1 %all-gather.1 = f32[66,8,128]{2,1,0:T(8,128)S(1)} all-gather(f32[33,8,128]{2,1,0:T(8,128)S(1)} %pad_maximum_fusion), channel_id=3, replica_groups=mesh['x'=4,'z'=12,'core'=2,'lev'=8] {'core'}, dimensions={0}, use_global_device_ids=true | all-gather | bytes 405504 | tf_op jit(solution)/shard_map/all_gather | solution.py:421
  35.9 0.0 copy-done.4
  35.9 0.0 copy-done.5
  35.9 0.0 copy-done.7
  36.0 0.0 copy-done.8
  36.0 0.0 copy-done.9
  36.0 2.6 %finish.1 = (f32[2,3072]{1,0:T(2,128)}, f32[2,3072]{1,0:T(2,128)}, f32[2,1024]{1,0:T(2,128)}) custom-call(s32[1]{0:T(128)} %bitcast.core_ref, f32[2,18,8,128]{3,2,1,0:T(8,128)S(1)} %bitcast.15, f32[2,33,8,128]{3,2,1,0:T(8,128)S(1)} %bitcast.16, f32[24,6,8,128]{3,2,1,0:T(8,128)S(1)} %get-tuple-element.9.sums_ref, ...), custom_call_target="tpu_custom_call" | custom-call | tf_op jit(solution)/shard_map/finish/pallas_call | solution.py:422
  (9 shorter events, 0.0 us)
Async XLA Ops:
  3.0 27.6 %copy-start.3 = (f32[6,1024]{1,0:T(8,128)S(1)}, f32[6,1024]{1,0:T(8,128)}, u32[]{:S(2)}) copy-start(f32[6,1024]{1,0:T(8,128)} %share_ref.3) | copy-start | bytes 73732
  3.0 27.6 %copy-start.6 = (f32[18,8,128]{2,1,0:T(8,128)S(1)}, f32[18,8,128]{2,1,0:T(8,128)}, u32[]{:S(2)}) copy-start(f32[18,8,128]{2,1,0:T(8,128)} %get-tuple-element.8.table_ref) | copy-start | bytes 221188
  5.6 25.1 %copy-start = (s32[10,3072]{1,0:T(8,128)S(1)}, s32[10,3072]{1,0:T(8,128)}, u32[]{:S(2)}) copy-start(s32[10,3072]{1,0:T(8,128)} %near_ref.3) | copy-start | bytes 368644
  5.6 25.1 %copy-start.1 = (f32[10,3072]{1,0:T(8,128)S(1)}, f32[10,3072]{1,0:T(8,128)}, u32[]{:S(2)}) copy-start(f32[10,3072]{1,0:T(8,128)} %weight_ref.3) | copy-start | bytes 368644
  5.6 28.1 %collective-permute-start = (f32[2,6,8,128]{3,2,1,0:T(8,128)S(1)}, f32[2,6,8,128]{3,2,1,0:T(8,128)S(1)}, u32[]{:S(2)}, u32[]{:S(2)}) collective-permute-start(f32[2,6,8,128]{3,2,1,0:T(8,128)S(1)} %slice_select_fusion), channel_id=1, source_target_pairs={{0,16},{16,32},{32,48},{48,64},{64,80},{80,96},{96,112},{112,128},... | collective-permute-start | bytes 147464 | tf_op jit(solution)/shard_map/ppermute | solution.py:394
  22.3 11.4 %collective-permute-start.1 = (f32[7,8,128]{2,1,0:T(8,128)S(1)}, f32[7,8,128]{2,1,0:T(8,128)S(1)}, u32[]{:S(2)}, u32[]{:S(2)}) collective-permute-start(f32[7,8,128]{2,1,0:T(8,128)S(1)} %pad_maximum_fusion.2), channel_id=1, source_target_pairs={{0,32},{16,48},{32,64},{48,80},{64,96},{80,112},{96,128},{112,144}... | collective-permute-start | bytes 86024 | tf_op jit(solution)/shard_map/ppermute | solution.py:394
  24.5 6.2 %copy-start.2 = (s32[6,1024]{1,0:T(8,128)S(1)}, s32[6,1024]{1,0:T(8,128)}, u32[]{:S(2)}) copy-start(s32[6,1024]{1,0:T(8,128)} %cells_ref.3) | copy-start | bytes 73732
  24.5 9.2 %collective-permute-start.2 = (f32[8,8,128]{2,1,0:T(8,128)S(1)}, f32[8,8,128]{2,1,0:T(8,128)S(1)}, u32[]{:S(2)}, u32[]{:S(2)}) collective-permute-start(f32[8,8,128]{2,1,0:T(8,128)S(1)} %pad_maximum_fusion.1), channel_id=1, source_target_pairs={{0,48},{16,64},{32,80},{48,96},{64,112},{80,128},{96,144},{112,160... | collective-permute-start | bytes 98312 | tf_op jit(solution)/shard_map/ppermute | solution.py:394
  27.6 6.1 %collective-permute-start.3 = (f32[2,3,8,128]{3,2,1,0:T(8,128)S(1)}, f32[2,3,8,128]{3,2,1,0:T(8,128)S(1)}, u32[]{:S(2)}, u32[]{:S(2)}) collective-permute-start(f32[2,3,8,128]{3,2,1,0:T(8,128)S(1)} %slice_select_fusion.1), channel_id=1, source_target_pairs={{0,1},{1,2},{2,3},{3,4},{4,5},{5,6},{6,7},{9,8},{10,9},{11,10},{12... | collective-permute-start | bytes 73736 | tf_op jit(solution)/shard_map/ppermute | solution.py:406
  33.7 2.2 %copy-start.4 = (f32[2,3072]{1,0:T(2,128)S(1)}, f32[2,3072]{1,0:T(2,128)}, u32[]{:S(2)}) copy-start(f32[2,3072]{1,0:T(2,128)} %speed_ref.1) | copy-start | bytes 73732
  33.8 2.2 %copy-start.5 = (f32[2,3072]{1,0:T(2,128)S(1)}, f32[2,3072]{1,0:T(2,128)}, u32[]{:S(2)}) copy-start(f32[2,3072]{1,0:T(2,128)} %vort_ref.1) | copy-start | bytes 73732
  33.8 2.2 %copy-start.7 = (s32[2,3072]{1,0:T(2,128)S(1)}, s32[2,3072]{1,0:T(2,128)}, u32[]{:S(2)}) copy-start(s32[2,3072]{1,0:T(2,128)} %ends_ref.1) | copy-start | bytes 73732
  33.8 2.2 %copy-start.8 = (f32[2,3072]{1,0:T(2,128)S(1)}, f32[2,3072]{1,0:T(2,128)}, u32[]{:S(2)}) copy-start(f32[2,3072]{1,0:T(2,128)} %wind_ref.1) | copy-start | bytes 73732
  33.8 2.2 %copy-start.9 = (f32[3072]{0:T(1024)S(1)}, f32[3072]{0:T(1024)}, u32[]{:S(2)}) copy-start(f32[3072]{0:T(1024)} %param.23) | copy-start | bytes 36868

commit v3 on v2

--- a/solution.py
+++ b/solution.py
@@ -34,7 +34,6 @@
 
 
 SPAN = 2 * LANES
-PRODUCTS = 9
 
 
 def split(table, axis):
@@ -162,22 +161,17 @@
         sums = [[jnp.zeros((8, LANES), jnp.float32) for _ in range(6)] for _ in range(2)]
         for side in range(10):
             index, weight = near_ref[side : side + 1, columns], weight_ref[side : side + 1, columns]
-            if side < PRODUCTS:
-                ones = ones_at(index, counts)
-                got = product(table, jnp.concatenate([ones, ones], axis=0))
+            ones = ones_at(index, counts)
+            got = product(table, jnp.concatenate([ones, ones], axis=0))
             for half in range(2):
                 part_of = slice(half * LANES, (half + 1) * LANES)
-                low, high = wide(index[:, part_of]) & 127, wide(index[:, part_of]) >> 7
+                high = wide(index[:, part_of]) >> 7
                 share = wide(weight[:, part_of])
                 for part in range(3):
                     here = jnp.where(high == spot + 8 * part, share, 0.0)
                     for field in range(6):
-                        tile = field * 3 + part
-                        if side < PRODUCTS:
-                            values = got[tile * 8 : tile * 8 + 8, part_of]
-                        else:
-                            values = pick(table_ref[tile], low)
-                        sums[half][field] = sums[half][field] + here * values
+                        row = (field * 3 + part) * 8
+                        sums[half][field] = sums[half][field] + here * got[row : row + 8, part_of]
         for half in range(2):
             for field in range(6):
                 sums_ref[step * 2 + half, field] = sums[half][field]
@@ -201,7 +195,7 @@
             energy_ref[step, level] = sums[level]
         return carry
 
-    lax.fori_loop(0, BLOCKS, cells, 0, unroll=4)
+    lax.fori_loop(0, BLOCKS, cells, 0, unroll=True)
 
 
 def finish_kernel(
@@ -377,9 +371,9 @@
         out_specs=(VMEM, VMEM),
         scratch_shapes=[pltpu.VMEM(x.shape, x.dtype) for x in inputs]
         + [pltpu.VMEM((8, LANES), jnp.int32), pltpu.SemaphoreType.DMA((7,))],
-        compiler_params=pltpu.CompilerParams(vmem_limit_bytes=60 << 20),
+        compiler_params=params,
         name="pack",
-    )(*inputs)
+    )(*(pltpu.with_memory_space_constraint(x, pltpu.HBM) for x in inputs))
 
     mesh_axes = ("x", "z", "core")
     own = lax.all_gather(sent, "core")

time: 39 us -> 37.7 us (0.967)
  the two profiles are of different devices: /device:TPU:57 before, /device:TPU:25 now
where the time goes in v3:
time: 37.7 us; the launch traced here: 37.3 us
  starting transfers between devices  24 us (64%)
  Pallas kernels  6.99 us (19%)
  blocking collectives  4.37 us (12%)
  waiting for transfers between devices  0.96 us (3%)
  between operations  0.86 us (2%)
    ppermute x3, starting transfers between devices, apart(): return lax.ppermute(block, mesh_axes, right + left)  21.9 us
    pallas_call x1, Pallas kernels, body(): pl.pallas_call(local_kernel, out_shape=(jax.ShapeDtypeStruct((ROWS, 6, 8,...  2.7 us
    pallas_call x1, Pallas kernels, body(): pl.pallas_call(finish_kernel, out_shape=(jax.ShapeDtypeStruct(velocity.sh...  2.57 us
    all_gather x1, blocking collectives, body(): own = lax.all_gather(sent, 'core')  2.23 us
    all_gather x1, blocking collectives, body(): around = lax.all_gather(arrived, 'core')  2.13 us
    ppermute x1, starting transfers between devices, body(): lax.ppermute(rims, ('core', 'lev'), up + down).reshape(6, 8, LANES)  2.08 us
    pallas_call x1, Pallas kernels, body(): pl.pallas_call(pack_kernel, out_shape=(jax.ShapeDtypeStruct((TILES, 8, LA...  1.72 us
    ppermute x1, waiting for transfers between devices, body(): lax.ppermute(rims, ('core', 'lev'), up + down).reshape(6, 8, LANES)  0.95 us
  transfers between devices with their start and end apart: 4, of which 1 were waited for; matrix products, arithmetic and copies ran while one was open for 0% of the time, Pallas kernels for 7%

profile of v3, /device:TPU:25, one launch (start us, length us, event | category | flops | bytes accessed | tf_op | source)
XLA Modules:
  0.0 37.3 jit_solution(16171504753399049832)
XLA Ops:
  0.6 1.7 %pack.1 = (f32[18,8,128]{2,1,0:T(8,128)S(1)}, f32[18,8,128]{2,1,0:T(8,128)S(1)}) custom-call(f32[2,3072]{1,0:T(2,128)} %speed_ref.1, f32[2,3072]{1,0:T(2,128)} %height_hbm.1, f32[2,3072]{1,0:T(2,128)} %vort_ref.1, s32[6,128]{1,0:T(8,128)} %edge_list_hbm.1, s32[6,64]{1,0:T(8,128)} %cell_list_hbm.1, s32[6,1024]{1,0:T(8,128)} %cells_ref.3, f32[6,1024]{1,0:T(8,128)} %share_ref.3), custom_call_target="tpu_custom_call" | custom-call | tf_op jit(solution)/shard_map/pack/pallas_call | solution.py:364
  2.4 0.0 copy-start.3
  2.4 2.2 %all-gather = f32[36,8,128]{2,1,0:T(8,128)S(1)} all-gather(f32[18,8,128]{2,1,0:T(8,128)S(1)} %get-tuple-element.7), channel_id=2, replica_groups=mesh['x'=4,'z'=12,'core'=2,'lev'=8] {'core'}, dimensions={0}, use_global_device_ids=true | all-gather | bytes 221184 | tf_op jit(solution)/shard_map/all_gather | solution.py:379
  4.6 0.0 copy-start
  4.6 0.0 copy-start.1
  4.6 16.6 %collective-permute-start = (f32[2,6,8,128]{3,2,1,0:T(8,128)S(1)}, f32[2,6,8,128]{3,2,1,0:T(8,128)S(1)}, u32[]{:S(2)}, u32[]{:S(2)}) collective-permute-start(f32[2,6,8,128]{3,2,1,0:T(8,128)S(1)} %slice_select_fusion), channel_id=1, source_target_pairs={{0,16},{16,32},{32,48},{48,64},{64,80},{80,96},{96,112},{112,128},... | collective-permute-start | bytes 147464 | tf_op jit(solution)/shard_map/ppermute | solution.py:388
  21.3 2.2 %collective-permute-start.1 = (f32[7,8,128]{2,1,0:T(8,128)S(1)}, f32[7,8,128]{2,1,0:T(8,128)S(1)}, u32[]{:S(2)}, u32[]{:S(2)}) collective-permute-start(f32[7,8,128]{2,1,0:T(8,128)S(1)} %pad_maximum_fusion.2), channel_id=1, source_target_pairs={{0,32},{16,48},{32,64},{48,80},{64,96},{80,112},{96,128},{112,144}... | collective-permute-start | bytes 86024 | tf_op jit(solution)/shard_map/ppermute | solution.py:388
  23.5 0.0 copy-start.2
  23.5 3.1 %collective-permute-start.2 = (f32[8,8,128]{2,1,0:T(8,128)S(1)}, f32[8,8,128]{2,1,0:T(8,128)S(1)}, u32[]{:S(2)}, u32[]{:S(2)}) collective-permute-start(f32[8,8,128]{2,1,0:T(8,128)S(1)} %pad_maximum_fusion.1), channel_id=1, source_target_pairs={{0,48},{16,64},{32,80},{48,96},{64,112},{80,128},{96,144},{112,160... | collective-permute-start | bytes 98312 | tf_op jit(solution)/shard_map/ppermute | solution.py:388
  26.7 2.1 %collective-permute-start.3 = (f32[2,3,8,128]{3,2,1,0:T(8,128)S(1)}, f32[2,3,8,128]{3,2,1,0:T(8,128)S(1)}, u32[]{:S(2)}, u32[]{:S(2)}) collective-permute-start(f32[2,3,8,128]{3,2,1,0:T(8,128)S(1)} %slice_select_fusion.1), channel_id=1, source_target_pairs={{0,1},{1,2},{2,3},{3,4},{4,5},{5,6},{6,7},{9,8},{10,9},{11,10},{12... | collective-permute-start | bytes 73736 | tf_op jit(solution)/shard_map/ppermute | solution.py:400
  28.7 0.0 copy-done.3
  28.8 0.0 copy-done
  28.8 0.0 copy-done.1
  28.8 0.0 copy-done.2
  28.8 2.7 %local.1 = (f32[24,6,8,128]{3,2,1,0:T(8,128)S(1)}, f32[8,2,8,128]{3,2,1,0:T(8,128)S(1)}) custom-call(f32[18,8,128]{2,1,0:T(8,128)S(1)} %get-tuple-element.8.table_ref, s32[10,3072]{1,0:T(8,128)S(1)} %copy-done, f32[10,3072]{1,0:T(8,128)S(1)} %copy-done.1, s32[6,1024]{1,0:T(8,128)S(1)} %copy-done.2, f32[6,1024]{1,0:T(8,128)S(1)} %copy-done.3), custom_call_target="tpu_custom_call" | custom-call | flops 20000000 | bytes 1000000 | tf_op jit(solution)/shard_map/local/pallas_call | solution.py:403
  31.5 0.9 %collective-permute-done.3 = f32[2,3,8,128]{3,2,1,0:T(8,128)S(1)} collective-permute-done((f32[2,3,8,128]{3,2,1,0:T(8,128)S(1)}, f32[2,3,8,128]{3,2,1,0:T(8,128)S(1)}, u32[]{:S(2)}, u32[]{:S(2)}) %collective-permute-start.3) | collective-permute-done | bytes 24608 | tf_op jit(solution)/shard_map/ppermute | solution.py:400
  32.4 0.0 collective-permute-done.1
  32.4 0.0 collective-permute-done.2
  32.4 0.0 collective-permute-done
  32.5 0.0 copy-start.4
  32.5 0.0 copy-start.5
  32.5 0.0 copy-start.6
  32.5 0.0 copy-start.7
  32.5 0.0 copy-start.8
  32.5 2.1 %all-gather.1 = f32[66,8,128]{2,1,0:T(8,128)S(1)} all-gather(f32[33,8,128]{2,1,0:T(8,128)S(1)} %pad_maximum_fusion), channel_id=3, replica_groups=mesh['x'=4,'z'=12,'core'=2,'lev'=8] {'core'}, dimensions={0}, use_global_device_ids=true | all-gather | bytes 405504 | tf_op jit(solution)/shard_map/all_gather | solution.py:415
  34.7 0.0 copy-done.4
  34.7 0.0 copy-done.5
  34.7 0.0 copy-done.6
  34.7 0.0 copy-done.7
  34.7 0.0 copy-done.8
  34.7 2.6 %finish.1 = (f32[2,3072]{1,0:T(2,128)}, f32[2,3072]{1,0:T(2,128)}, f32[2,1024]{1,0:T(2,128)}) custom-call(s32[1]{0:T(128)} %bitcast.core_ref, f32[2,18,8,128]{3,2,1,0:T(8,128)S(1)} %bitcast.15, f32[2,33,8,128]{3,2,1,0:T(8,128)S(1)} %bitcast.16, f32[24,6,8,128]{3,2,1,0:T(8,128)S(1)} %get-tuple-element.9.sums_ref, ...), custom_call_target="tpu_custom_call" | custom-call | tf_op jit(solution)/shard_map/finish/pallas_call | solution.py:416
  (9 shorter events, 0.0 us)
Async XLA Ops:
  2.4 26.4 %copy-start.3 = (f32[6,1024]{1,0:T(8,128)S(1)}, f32[6,1024]{1,0:T(8,128)}, u32[]{:S(2)}) copy-start(f32[6,1024]{1,0:T(8,128)} %share_ref.3) | copy-start | bytes 73732
  4.6 24.1 %copy-start = (s32[10,3072]{1,0:T(8,128)S(1)}, s32[10,3072]{1,0:T(8,128)}, u32[]{:S(2)}) copy-start(s32[10,3072]{1,0:T(8,128)} %near_ref.3) | copy-start | bytes 368644
  4.6 24.2 %copy-start.1 = (f32[10,3072]{1,0:T(8,128)S(1)}, f32[10,3072]{1,0:T(8,128)}, u32[]{:S(2)}) copy-start(f32[10,3072]{1,0:T(8,128)} %weight_ref.3) | copy-start | bytes 368644
  4.6 27.8 %collective-permute-start = (f32[2,6,8,128]{3,2,1,0:T(8,128)S(1)}, f32[2,6,8,128]{3,2,1,0:T(8,128)S(1)}, u32[]{:S(2)}, u32[]{:S(2)}) collective-permute-start(f32[2,6,8,128]{3,2,1,0:T(8,128)S(1)} %slice_select_fusion), channel_id=1, source_target_pairs={{0,16},{16,32},{32,48},{48,64},{64,80},{80,96},{96,112},{112,128},... | collective-permute-start | bytes 147464 | tf_op jit(solution)/shard_map/ppermute | solution.py:388
  21.3 11.1 %collective-permute-start.1 = (f32[7,8,128]{2,1,0:T(8,128)S(1)}, f32[7,8,128]{2,1,0:T(8,128)S(1)}, u32[]{:S(2)}, u32[]{:S(2)}) collective-permute-start(f32[7,8,128]{2,1,0:T(8,128)S(1)} %pad_maximum_fusion.2), channel_id=1, source_target_pairs={{0,32},{16,48},{32,64},{48,80},{64,96},{80,112},{96,128},{112,144}... | collective-permute-start | bytes 86024 | tf_op jit(solution)/shard_map/ppermute | solution.py:388
  23.5 5.3 %copy-start.2 = (s32[6,1024]{1,0:T(8,128)S(1)}, s32[6,1024]{1,0:T(8,128)}, u32[]{:S(2)}) copy-start(s32[6,1024]{1,0:T(8,128)} %cells_ref.3) | copy-start | bytes 73732
  23.5 8.9 %collective-permute-start.2 = (f32[8,8,128]{2,1,0:T(8,128)S(1)}, f32[8,8,128]{2,1,0:T(8,128)S(1)}, u32[]{:S(2)}, u32[]{:S(2)}) collective-permute-start(f32[8,8,128]{2,1,0:T(8,128)S(1)} %pad_maximum_fusion.1), channel_id=1, source_target_pairs={{0,48},{16,64},{32,80},{48,96},{64,112},{80,128},{96,144},{112,160... | collective-permute-start | bytes 98312 | tf_op jit(solution)/shard_map/ppermute | solution.py:388
  26.7 5.8 %collective-permute-start.3 = (f32[2,3,8,128]{3,2,1,0:T(8,128)S(1)}, f32[2,3,8,128]{3,2,1,0:T(8,128)S(1)}, u32[]{:S(2)}, u32[]{:S(2)}) collective-permute-start(f32[2,3,8,128]{3,2,1,0:T(8,128)S(1)} %slice_select_fusion.1), channel_id=1, source_target_pairs={{0,1},{1,2},{2,3},{3,4},{4,5},{5,6},{6,7},{9,8},{10,9},{11,10},{12... | collective-permute-start | bytes 73736 | tf_op jit(solution)/shard_map/ppermute | solution.py:400
  32.5 2.2 %copy-start.4 = (f32[2,3072]{1,0:T(2,128)S(1)}, f32[2,3072]{1,0:T(2,128)}, u32[]{:S(2)}) copy-start(f32[2,3072]{1,0:T(2,128)} %speed_ref.1) | copy-start | bytes 73732
  32.5 2.2 %copy-start.5 = (f32[2,3072]{1,0:T(2,128)S(1)}, f32[2,3072]{1,0:T(2,128)}, u32[]{:S(2)}) copy-start(f32[2,3072]{1,0:T(2,128)} %vort_ref.1) | copy-start | bytes 73732
  32.5 2.2 %copy-start.6 = (s32[2,3072]{1,0:T(2,128)S(1)}, s32[2,3072]{1,0:T(2,128)}, u32[]{:S(2)}) copy-start(s32[2,3072]{1,0:T(2,128)} %ends_ref.1) | copy-start | bytes 73732
  32.5 2.2 %copy-start.7 = (f32[2,3072]{1,0:T(2,128)S(1)}, f32[2,3072]{1,0:T(2,128)}, u32[]{:S(2)}) copy-start(f32[2,3072]{1,0:T(2,128)} %wind_ref.1) | copy-start | bytes 73732
  32.5 2.2 %copy-start.8 = (f32[3072]{0:T(1024)S(1)}, f32[3072]{0:T(1024)}, u32[]{:S(2)}) copy-start(f32[3072]{0:T(1024)} %param.23) | copy-start | bytes 36868

commit v4 on v3

--- a/solution.py
+++ b/solution.py
@@ -14,7 +14,8 @@
 WAY = 6
 RIM = 2 * WAY
 TILES = RIM + 6
-NEAR, MIDDLE, FAR, EDGE = 0, 12, 19, 27
+EARLY = 4
+NEAR, MIDDLE, FAR, EDGE = 0, 12, 20, 27
 
 
 def pick(table, low):
@@ -149,9 +150,27 @@
             sent_ref[way + place // 2, row : row + 1, :] = parts[half]
 
 
-def local_kernel(
-    table_ref, near_ref, weight_ref, cells_ref, share_ref, sums_ref, energy_ref,
+def local_early_kernel(early_ref, table_ref, near_ref, weight_ref, sums_ref):
+    @pl.when(early_ref[0] == 1)
+    def _():
+        local_sums(table_ref, near_ref, weight_ref, sums_ref)
+
+
+def local_late_kernel(
+    early_ref, made_ref, table_ref, near_ref, weight_ref, cells_ref, share_ref, sums_ref, energy_ref,
 ):
+    @pl.when(early_ref[0] == 1)
+    def _():
+        sums_ref[...] = made_ref[...]
+        cell_sums(table_ref, cells_ref, share_ref, energy_ref)
+
+    @pl.when(early_ref[0] == 0)
+    def _():
+        local_sums(table_ref, near_ref, weight_ref, sums_ref)
+        cell_sums(table_ref, cells_ref, share_ref, energy_ref)
+
+
+def local_sums(table_ref, near_ref, weight_ref, sums_ref):
     spot = sublanes()
     table = split(table_ref[...].reshape(18 * 8, LANES), 1)
     counts = counting()
@@ -178,6 +197,10 @@
         return carry
 
     lax.fori_loop(0, ROWS // 2, edges, 0, unroll=True)
+
+
+def cell_sums(table_ref, cells_ref, share_ref, energy_ref):
+    spot = sublanes()
 
     def cells(step, carry):
         columns = pl.ds(pl.multiple_of(step * LANES, LANES), LANES)
@@ -378,6 +401,22 @@
     mesh_axes = ("x", "z", "core")
     own = lax.all_gather(sent, "core")
     even = core == 0
+    z = lax.axis_index("z")
+    corner = lax.axis_index("x") + lax.axis_index("lev") + z == 0
+    early = ((z < EARLY) & ~corner).astype(jnp.int32).reshape(1)
+    own, tables = lax.optimization_barrier((own, tables))
+    operands = (tables, edges_on_edge, weights_on_edge)
+    flag = pl.BlockSpec(memory_space=pltpu.SMEM)
+    sums_shape = jax.ShapeDtypeStruct((ROWS, 6, 8, LANES), f32)
+    made = pl.pallas_call(
+        local_early_kernel,
+        out_shape=sums_shape,
+        in_specs=[flag] + [VMEM] * 3,
+        out_specs=VMEM,
+        compiler_params=params,
+        name="local_early",
+    )(early, *operands)
+    own, made = lax.optimization_barrier((own, made))
     near = jnp.where(even, own[:, :WAY], own[:, WAY:RIM])
     rims = jnp.where(even, own[:, RIM + 3 :], own[:, RIM : RIM + 3])
     chips = lax.axis_size("x") * lax.axis_size("z")
@@ -395,23 +434,20 @@
     spare = near[1]
     arrived = [
         apart(near, 1).reshape(12, 8, LANES),
-        apart(jnp.concatenate([speeds, rest, spare[:1]], axis=0), 2),
-        apart(jnp.concatenate([speeds, spare[:4]], axis=0), 3),
+        apart(jnp.concatenate([speeds, rest, spare[:2]], axis=0), 2),
+        apart(jnp.concatenate([speeds, spare[:3]], axis=0), 3),
         lax.ppermute(rims, ("core", "lev"), up + down).reshape(6, 8, LANES),
     ]
     arrived = jnp.concatenate(arrived, axis=0)
     sums, energy_sums = pl.pallas_call(
-        local_kernel,
-        out_shape=(
-            jax.ShapeDtypeStruct((ROWS, 6, 8, LANES), f32),
-            jax.ShapeDtypeStruct((BLOCKS, 2, 8, LANES), f32),
-        ),
-        in_specs=[VMEM] * 5,
+        local_late_kernel,
+        out_shape=(sums_shape, jax.ShapeDtypeStruct((BLOCKS, 2, 8, LANES), f32)),
+        in_specs=[flag] + [VMEM] * 6,
         out_specs=(VMEM, VMEM),
         compiler_params=params,
         cost_estimate=pl.CostEstimate(flops=20_000_000, bytes_accessed=1_000_000, transcendentals=0),
-        name="local",
-    )(tables, edges_on_edge, weights_on_edge, edges_on_cell, energy_weight)
+        name="local_late",
+    )(early, made, *operands, edges_on_cell, energy_weight)
     around = lax.all_gather(arrived, "core")
     return pl.pallas_call(
         finish_kernel,

time: 37.7 us -> 37.5 us (level)
  starting transfers between devices: 24 us -> 21.3 us
  waiting for transfers between devices: 0.96 us -> 3.14 us
    ppermute x3, starting transfers between devices: 21.9 us -> 19.3 us  [apart(): return lax.ppermute(block, mesh_axes, right + left)]
    ppermute x1, waiting for transfers between devices: 0.95 us -> 3.13 us  [body(): lax.ppermute(rims, ('core', 'lev'), up + down).reshape(6, 8, LANES)]
    pallas_call x1 -> x2, Pallas kernels: 2.7 us -> 3.03 us  [the longest x1 2.5 us: body(): pl.pallas_call(local_early_kernel, out_shape=sums_shape, in_specs=[flag]...]
  transfers between devices with their start and end apart: 4 -> 4, of which waited for: 1 -> 1; matrix products, arithmetic and copies ran while one was open for 0% -> 0% of each run, Pallas kernels for 7% -> 1%
where the time goes in v4:
time: 37.5 us; the launch traced here: 37.2 us
  starting transfers between devices  21.3 us (57%)
  Pallas kernels  7.36 us (20%)
  blocking collectives  4.37 us (12%)
  waiting for transfers between devices  3.14 us (8%)
  between operations  0.89 us (2%)
    ppermute x3, starting transfers between devices, apart(): return lax.ppermute(block, mesh_axes, right + left)  19.3 us
    ppermute x1, waiting for transfers between devices, body(): lax.ppermute(rims, ('core', 'lev'), up + down).reshape(6, 8, LANES)  3.13 us
    pallas_call x1, Pallas kernels, body(): pl.pallas_call(finish_kernel, out_shape=(jax.ShapeDtypeStruct(velocity.sh...  2.55 us
    pallas_call x1, Pallas kernels, body(): pl.pallas_call(local_early_kernel, out_shape=sums_shape, in_specs=[flag]...  2.5 us
    all_gather x1, blocking collectives, body(): own = lax.all_gather(sent, 'core')  2.23 us
    all_gather x1, blocking collectives, body(): around = lax.all_gather(arrived, 'core')  2.13 us
    ppermute x1, starting transfers between devices, body(): lax.ppermute(rims, ('core', 'lev'), up + down).reshape(6, 8, LANES)  2.08 us
    pallas_call x1, Pallas kernels, body(): pl.pallas_call(pack_kernel, out_shape=(jax.ShapeDtypeStruct((TILES, 8, LA...  1.77 us
  transfers between devices with their start and end apart: 4, of which 1 were waited for; matrix products, arithmetic and copies ran while one was open for 0% of the time, Pallas kernels for 1%

profile of v4, /device:TPU:25, one launch (start us, length us, event | category | flops | bytes accessed | tf_op | source)
XLA Modules:
  0.0 37.2 jit_solution(4096863994512503812)
XLA Ops:
  0.6 0.0 copy-start
  0.7 0.0 copy-start.1
  0.7 1.8 %pack.1 = (f32[18,8,128]{2,1,0:T(8,128)S(1)}, f32[18,8,128]{2,1,0:T(8,128)S(1)}) custom-call(f32[2,3072]{1,0:T(2,128)} %speed_ref.1, f32[2,3072]{1,0:T(2,128)} %height_hbm.1, f32[2,3072]{1,0:T(2,128)} %vort_ref.1, s32[6,128]{1,0:T(8,128)} %edge_list_hbm.1, s32[6,64]{1,0:T(8,128)} %cell_list_hbm.1, s32[6,1024]{1,0:T(8,128)} %cells_ref.3, f32[6,1024]{1,0:T(8,128)} %share_ref.3), custom_call_target="tpu_custom_call" | custom-call | tf_op jit(solution)/shard_map/pack/pallas_call | solution.py:387
  2.5 2.2 %all-gather = f32[36,8,128]{2,1,0:T(8,128)S(1)} all-gather(f32[18,8,128]{2,1,0:T(8,128)S(1)} %get-tuple-element.11), channel_id=2, replica_groups=mesh['x'=4,'z'=12,'core'=2,'lev'=8] {'core'}, dimensions={0}, use_global_device_ids=true | all-gather | bytes 221184 | tf_op jit(solution)/shard_map/all_gather | solution.py:402
  4.7 0.0 copy-done
  4.7 0.0 copy-done.1
  4.7 2.5 %local_early.1.made_ref = f32[24,6,8,128]{3,2,1,0:T(8,128)S(1)} custom-call(s32[1]{0:T(128)} %bitcast.2.early_ref, f32[18,8,128]{2,1,0:T(8,128)S(1)} %get-tuple-element.14.table_ref, s32[10,3072]{1,0:T(8,128)S(1)} %copy-done, f32[10,3072]{1,0:T(8,128)S(1)} %copy-done.1), custom_call_target="tpu_custom_call" | custom-call | tf_op jit(solution)/shard_map/local_early/pallas_call | solution.py:411
  7.2 14.0 %collective-permute-start = (f32[2,6,8,128]{3,2,1,0:T(8,128)S(1)}, f32[2,6,8,128]{3,2,1,0:T(8,128)S(1)}, u32[]{:S(2)}, u32[]{:S(2)}) collective-permute-start(f32[2,6,8,128]{3,2,1,0:T(8,128)S(1)} %slice_select_fusion), channel_id=1, source_target_pairs={{0,16},{16,32},{32,48},{48,64},{64,80},{80,96},{96,112},{112,128},... | collective-permute-start | bytes 147464 | tf_op jit(solution)/shard_map/ppermute | solution.py:427
  21.3 2.2 %collective-permute-start.2 = (f32[7,8,128]{2,1,0:T(8,128)S(1)}, f32[7,8,128]{2,1,0:T(8,128)S(1)}, u32[]{:S(2)}, u32[]{:S(2)}) collective-permute-start(f32[7,8,128]{2,1,0:T(8,128)S(1)} %pad_maximum_fusion.2), channel_id=1, source_target_pairs={{0,48},{16,64},{32,80},{48,96},{64,112},{80,128},{96,144},{112,160... | collective-permute-start | bytes 86024 | tf_op jit(solution)/shard_map/ppermute | solution.py:427
  23.4 0.0 copy-start.2
  23.5 0.0 copy-start.3
  23.5 3.1 %collective-permute-start.1 = (f32[8,8,128]{2,1,0:T(8,128)S(1)}, f32[8,8,128]{2,1,0:T(8,128)S(1)}, u32[]{:S(2)}, u32[]{:S(2)}) collective-permute-start(f32[8,8,128]{2,1,0:T(8,128)S(1)} %pad_maximum_fusion.1), channel_id=1, source_target_pairs={{0,32},{16,48},{32,64},{48,80},{64,96},{80,112},{96,128},{112,144}... | collective-permute-start | bytes 98312 | tf_op jit(solution)/shard_map/ppermute | solution.py:427
  26.6 2.1 %collective-permute-start.3 = (f32[2,3,8,128]{3,2,1,0:T(8,128)S(1)}, f32[2,3,8,128]{3,2,1,0:T(8,128)S(1)}, u32[]{:S(2)}, u32[]{:S(2)}) collective-permute-start(f32[2,3,8,128]{3,2,1,0:T(8,128)S(1)} %slice_select_fusion.1), channel_id=1, source_target_pairs={{0,1},{1,2},{2,3},{3,4},{4,5},{5,6},{6,7},{9,8},{10,9},{11,10},{12... | collective-permute-start | bytes 73736 | tf_op jit(solution)/shard_map/ppermute | solution.py:439
  28.7 0.0 copy-done.2
  28.7 0.0 copy-done.3
  28.7 0.5 %local_late.1 = (f32[24,6,8,128]{3,2,1,0:T(8,128)S(1)}, f32[8,2,8,128]{3,2,1,0:T(8,128)S(1)}) custom-call(s32[1]{0:T(128)} %bitcast.2.early_ref, f32[24,6,8,128]{3,2,1,0:T(8,128)S(1)} %local_early.1.made_ref, f32[18,8,128]{2,1,0:T(8,128)S(1)} %get-tuple-element.14.table_ref, s32[10,3072]{1,0:T(8,128)S(1)} %copy-done, f32[10,3072]{1,0:T(8,128)S(1)} %copy-done.1, ...), custom_call_target="tpu_custom_call" | custom-call | flops 20000000 | bytes 1000000 | tf_op jit(solution)/shard_map/local_late/pallas_call | solution.py:442
  29.3 3.1 %collective-permute-done.3 = f32[2,3,8,128]{3,2,1,0:T(8,128)S(1)} collective-permute-done((f32[2,3,8,128]{3,2,1,0:T(8,128)S(1)}, f32[2,3,8,128]{3,2,1,0:T(8,128)S(1)}, u32[]{:S(2)}, u32[]{:S(2)}) %collective-permute-start.3) | collective-permute-done | bytes 24608 | tf_op jit(solution)/shard_map/ppermute | solution.py:439
  32.4 0.0 collective-permute-done.2
  32.4 0.0 collective-permute-done.1
  32.4 0.0 collective-permute-done
  32.4 0.0 copy-start.4
  32.4 0.0 copy-start.5
  32.5 0.0 copy-start.6
  32.5 0.0 copy-start.7
  32.5 0.0 copy-start.8
  32.5 2.1 %all-gather.1 = f32[66,8,128]{2,1,0:T(8,128)S(1)} all-gather(f32[33,8,128]{2,1,0:T(8,128)S(1)} %pad_maximum_fusion), channel_id=3, replica_groups=mesh['x'=4,'z'=12,'core'=2,'lev'=8] {'core'}, dimensions={0}, use_global_device_ids=true | all-gather | bytes 405504 | tf_op jit(solution)/shard_map/all_gather | solution.py:451
  34.6 0.0 copy-done.4
  34.6 0.0 copy-done.5
  34.6 0.0 copy-done.6
  34.6 0.0 copy-done.7
  34.6 0.0 copy-done.8
  34.7 2.6 %finish.1 = (f32[2,3072]{1,0:T(2,128)}, f32[2,3072]{1,0:T(2,128)}, f32[2,1024]{1,0:T(2,128)}) custom-call(s32[1]{0:T(128)} %bitcast.core_ref, f32[2,18,8,128]{3,2,1,0:T(8,128)S(1)} %bitcast.16, f32[2,33,8,128]{3,2,1,0:T(8,128)S(1)} %bitcast.17, f32[24,6,8,128]{3,2,1,0:T(8,128)S(1)} %get-tuple-element.17.sums_ref, ...), custom_call_target="tpu_custom_call" | custom-call | tf_op jit(solution)/shard_map/finish/pallas_call | solution.py:452
  (8 shorter events, 0.0 us)
Async XLA Ops:
  0.6 4.1 %copy-start = (s32[10,3072]{1,0:T(8,128)S(1)}, s32[10,3072]{1,0:T(8,128)}, u32[]{:S(2)}) copy-start(s32[10,3072]{1,0:T(8,128)} %near_ref.5) | copy-start | bytes 368644
  0.7 4.0 %copy-start.1 = (f32[10,3072]{1,0:T(8,128)S(1)}, f32[10,3072]{1,0:T(8,128)}, u32[]{:S(2)}) copy-start(f32[10,3072]{1,0:T(8,128)} %weight_ref.5) | copy-start | bytes 368644
  7.2 25.2 %collective-permute-start = (f32[2,6,8,128]{3,2,1,0:T(8,128)S(1)}, f32[2,6,8,128]{3,2,1,0:T(8,128)S(1)}, u32[]{:S(2)}, u32[]{:S(2)}) collective-permute-start(f32[2,6,8,128]{3,2,1,0:T(8,128)S(1)} %slice_select_fusion), channel_id=1, source_target_pairs={{0,16},{16,32},{32,48},{48,64},{64,80},{80,96},{96,112},{112,128},... | collective-permute-start | bytes 147464 | tf_op jit(solution)/shard_map/ppermute | solution.py:427
  21.3 11.1 %collective-permute-start.2 = (f32[7,8,128]{2,1,0:T(8,128)S(1)}, f32[7,8,128]{2,1,0:T(8,128)S(1)}, u32[]{:S(2)}, u32[]{:S(2)}) collective-permute-start(f32[7,8,128]{2,1,0:T(8,128)S(1)} %pad_maximum_fusion.2), channel_id=1, source_target_pairs={{0,48},{16,64},{32,80},{48,96},{64,112},{80,128},{96,144},{112,160... | collective-permute-start | bytes 86024 | tf_op jit(solution)/shard_map/ppermute | solution.py:427
  23.4 5.3 %copy-start.2 = (s32[6,1024]{1,0:T(8,128)S(1)}, s32[6,1024]{1,0:T(8,128)}, u32[]{:S(2)}) copy-start(s32[6,1024]{1,0:T(8,128)} %cells_ref.3) | copy-start | bytes 73732
  23.5 5.3 %copy-start.3 = (f32[6,1024]{1,0:T(8,128)S(1)}, f32[6,1024]{1,0:T(8,128)}, u32[]{:S(2)}) copy-start(f32[6,1024]{1,0:T(8,128)} %share_ref.3) | copy-start | bytes 73732
  23.5 8.9 %collective-permute-start.1 = (f32[8,8,128]{2,1,0:T(8,128)S(1)}, f32[8,8,128]{2,1,0:T(8,128)S(1)}, u32[]{:S(2)}, u32[]{:S(2)}) collective-permute-start(f32[8,8,128]{2,1,0:T(8,128)S(1)} %pad_maximum_fusion.1), channel_id=1, source_target_pairs={{0,32},{16,48},{32,64},{48,80},{64,96},{80,112},{96,128},{112,144}... | collective-permute-start | bytes 98312 | tf_op jit(solution)/shard_map/ppermute | solution.py:427
  26.6 5.8 %collective-permute-start.3 = (f32[2,3,8,128]{3,2,1,0:T(8,128)S(1)}, f32[2,3,8,128]{3,2,1,0:T(8,128)S(1)}, u32[]{:S(2)}, u32[]{:S(2)}) collective-permute-start(f32[2,3,8,128]{3,2,1,0:T(8,128)S(1)} %slice_select_fusion.1), channel_id=1, source_target_pairs={{0,1},{1,2},{2,3},{3,4},{4,5},{5,6},{6,7},{9,8},{10,9},{11,10},{12... | collective-permute-start | bytes 73736 | tf_op jit(solution)/shard_map/ppermute | solution.py:439
  32.4 2.2 %copy-start.4 = (f32[2,3072]{1,0:T(2,128)S(1)}, f32[2,3072]{1,0:T(2,128)}, u32[]{:S(2)}) copy-start(f32[2,3072]{1,0:T(2,128)} %speed_ref.1) | copy-start | bytes 73732
  32.4 2.2 %copy-start.5 = (f32[2,3072]{1,0:T(2,128)S(1)}, f32[2,3072]{1,0:T(2,128)}, u32[]{:S(2)}) copy-start(f32[2,3072]{1,0:T(2,128)} %vort_ref.1) | copy-start | bytes 73732
  32.5 2.2 %copy-start.6 = (s32[2,3072]{1,0:T(2,128)S(1)}, s32[2,3072]{1,0:T(2,128)}, u32[]{:S(2)}) copy-start(s32[2,3072]{1,0:T(2,128)} %ends_ref.1) | copy-start | bytes 73732
  32.5 2.2 %copy-start.7 = (f32[2,3072]{1,0:T(2,128)S(1)}, f32[2,3072]{1,0:T(2,128)}, u32[]{:S(2)}) copy-start(f32[2,3072]{1,0:T(2,128)} %wind_ref.1) | copy-start | bytes 73732
  32.5 2.2 %copy-start.8 = (f32[3072]{0:T(1024)S(1)}, f32[3072]{0:T(1024)}, u32[]{:S(2)}) copy-start(f32[3072]{0:T(1024)} %param.23) | copy-start | bytes 36868

commit v5 on v4

--- a/solution.py
+++ b/solution.py
@@ -78,7 +78,10 @@
     copies = [pltpu.make_async_copy(src, dst, done.at[i]) for i, (src, dst) in enumerate(pairs)]
     for copy in copies:
         copy.start()
-    for copy in copies:
+    for way in range(2):
+        for tile in (0, 1, 5):
+            sent_ref[way * WAY + tile] = jnp.zeros((8, LANES), jnp.float32)
+    for copy in copies[:3]:
         copy.wait()
     for level in range(2):
         for row in range(ROWS):
@@ -93,10 +96,8 @@
         table_ref[6 + tile] = mass
         table_ref[12 + tile] = mass * table_ref[12 + tile]
         sent_ref[RIM + tile] = speed
-    for way in range(2):
-        for tile in (0, 1, 5):
-            sent_ref[way * WAY + tile] = jnp.zeros((8, LANES), jnp.float32)
     spot = sublanes()
+    copies[3].wait()
     for block in range(6):
         index = wide(edge_list_ref[block : block + 1, :])
         low, high = index & 127, index >> 7
@@ -114,6 +115,8 @@
                 sent_ref[way + 2 + place, 6 + level : 7 + level, :] = row
             else:
                 sent_ref[way + 5, level * 3 + place : level * 3 + place + 1, :] = row
+    for copy in copies[4:]:
+        copy.wait()
     pair_ref[...] = jnp.zeros((8, LANES), jnp.int32)
     for block in range(6):
         pair_ref[block : block + 1, 0:64] = cell_list_ref[block : block + 1, :]

time: 37.5 us -> 37.4 us (level)
  no operation moved by 1% of the time
where the time goes in v5:
time: 37.4 us; the launch traced here: 37.1 us
  starting transfers between devices  21.4 us (57%)
  Pallas kernels  7.24 us (19%)
  blocking collectives  4.37 us (12%)
  waiting for transfers between devices  3.14 us (8%)
  between operations  0.89 us (2%)
    ppermute x3, starting transfers between devices, apart(): return lax.ppermute(block, mesh_axes, right + left)  19.3 us
    ppermute x1, waiting for transfers between devices, body(): lax.ppermute(rims, ('core', 'lev'), up + down).reshape(6, 8, LANES)  3.13 us
    pallas_call x1, Pallas kernels, body(): pl.pallas_call(finish_kernel, out_shape=(jax.ShapeDtypeStruct(velocity.sh...  2.55 us
    pallas_call x1, Pallas kernels, body(): pl.pallas_call(local_early_kernel, out_shape=sums_shape, in_specs=[flag]...  2.49 us
    all_gather x1, blocking collectives, body(): own = lax.all_gather(sent, 'core')  2.23 us
    all_gather x1, blocking collectives, body(): around = lax.all_gather(arrived, 'core')  2.13 us
    ppermute x1, starting transfers between devices, body(): lax.ppermute(rims, ('core', 'lev'), up + down).reshape(6, 8, LANES)  2.08 us
    pallas_call x1, Pallas kernels, body(): pl.pallas_call(pack_kernel, out_shape=(jax.ShapeDtypeStruct((TILES, 8, LA...  1.67 us
  transfers between devices with their start and end apart: 4, of which 1 were waited for; matrix products, arithmetic and copies ran while one was open for 0% of the time, Pallas kernels for 1%

profile of v5, /device:TPU:25, one launch (start us, length us, event | category | flops | bytes accessed | tf_op | source)
XLA Modules:
  0.0 37.1 jit_solution(6477420337130443238)
XLA Ops:
  0.6 0.0 copy-start
  0.7 0.0 copy-start.1
  0.7 1.7 %pack.1 = (f32[18,8,128]{2,1,0:T(8,128)S(1)}, f32[18,8,128]{2,1,0:T(8,128)S(1)}) custom-call(f32[2,3072]{1,0:T(2,128)} %speed_ref.1, f32[2,3072]{1,0:T(2,128)} %height_hbm.1, f32[2,3072]{1,0:T(2,128)} %vort_ref.1, s32[6,128]{1,0:T(8,128)} %edge_list_hbm.1, s32[6,64]{1,0:T(8,128)} %cell_list_hbm.1, s32[6,1024]{1,0:T(8,128)} %cells_ref.3, f32[6,1024]{1,0:T(8,128)} %share_ref.3), custom_call_target="tpu_custom_call" | custom-call | tf_op jit(solution)/shard_map/pack/pallas_call | solution.py:390
  2.4 2.2 %all-gather = f32[36,8,128]{2,1,0:T(8,128)S(1)} all-gather(f32[18,8,128]{2,1,0:T(8,128)S(1)} %get-tuple-element.11), channel_id=2, replica_groups=mesh['x'=4,'z'=12,'core'=2,'lev'=8] {'core'}, dimensions={0}, use_global_device_ids=true | all-gather | bytes 221184 | tf_op jit(solution)/shard_map/all_gather | solution.py:405
  4.6 0.0 copy-done
  4.6 0.0 copy-done.1
  4.6 2.5 %local_early.1.made_ref = f32[24,6,8,128]{3,2,1,0:T(8,128)S(1)} custom-call(s32[1]{0:T(128)} %bitcast.2.early_ref, f32[18,8,128]{2,1,0:T(8,128)S(1)} %get-tuple-element.14.table_ref, s32[10,3072]{1,0:T(8,128)S(1)} %copy-done, f32[10,3072]{1,0:T(8,128)S(1)} %copy-done.1), custom_call_target="tpu_custom_call" | custom-call | tf_op jit(solution)/shard_map/local_early/pallas_call | solution.py:414
  7.1 14.0 %collective-permute-start = (f32[2,6,8,128]{3,2,1,0:T(8,128)S(1)}, f32[2,6,8,128]{3,2,1,0:T(8,128)S(1)}, u32[]{:S(2)}, u32[]{:S(2)}) collective-permute-start(f32[2,6,8,128]{3,2,1,0:T(8,128)S(1)} %slice_select_fusion), channel_id=1, source_target_pairs={{0,16},{16,32},{32,48},{48,64},{64,80},{80,96},{96,112},{112,128},... | collective-permute-start | bytes 147464 | tf_op jit(solution)/shard_map/ppermute | solution.py:430
  21.1 2.2 %collective-permute-start.2 = (f32[7,8,128]{2,1,0:T(8,128)S(1)}, f32[7,8,128]{2,1,0:T(8,128)S(1)}, u32[]{:S(2)}, u32[]{:S(2)}) collective-permute-start(f32[7,8,128]{2,1,0:T(8,128)S(1)} %pad_maximum_fusion.2), channel_id=1, source_target_pairs={{0,48},{16,64},{32,80},{48,96},{64,112},{80,128},{96,144},{112,160... | collective-permute-start | bytes 86024 | tf_op jit(solution)/shard_map/ppermute | solution.py:430
  23.3 0.0 copy-start.2
  23.4 0.0 copy-start.3
  23.4 3.1 %collective-permute-start.1 = (f32[8,8,128]{2,1,0:T(8,128)S(1)}, f32[8,8,128]{2,1,0:T(8,128)S(1)}, u32[]{:S(2)}, u32[]{:S(2)}) collective-permute-start(f32[8,8,128]{2,1,0:T(8,128)S(1)} %pad_maximum_fusion.1), channel_id=1, source_target_pairs={{0,32},{16,48},{32,64},{48,80},{64,96},{80,112},{96,128},{112,144}... | collective-permute-start | bytes 98312 | tf_op jit(solution)/shard_map/ppermute | solution.py:430
  26.5 2.1 %collective-permute-start.3 = (f32[2,3,8,128]{3,2,1,0:T(8,128)S(1)}, f32[2,3,8,128]{3,2,1,0:T(8,128)S(1)}, u32[]{:S(2)}, u32[]{:S(2)}) collective-permute-start(f32[2,3,8,128]{3,2,1,0:T(8,128)S(1)} %slice_select_fusion.1), channel_id=1, source_target_pairs={{0,1},{1,2},{2,3},{3,4},{4,5},{5,6},{6,7},{9,8},{10,9},{11,10},{12... | collective-permute-start | bytes 73736 | tf_op jit(solution)/shard_map/ppermute | solution.py:442
  28.6 0.0 copy-done.2
  28.6 0.0 copy-done.3
  28.6 0.5 %local_late.1 = (f32[24,6,8,128]{3,2,1,0:T(8,128)S(1)}, f32[8,2,8,128]{3,2,1,0:T(8,128)S(1)}) custom-call(s32[1]{0:T(128)} %bitcast.2.early_ref, f32[24,6,8,128]{3,2,1,0:T(8,128)S(1)} %local_early.1.made_ref, f32[18,8,128]{2,1,0:T(8,128)S(1)} %get-tuple-element.14.table_ref, s32[10,3072]{1,0:T(8,128)S(1)} %copy-done, f32[10,3072]{1,0:T(8,128)S(1)} %copy-done.1, ...), custom_call_target="tpu_custom_call" | custom-call | flops 20000000 | bytes 1000000 | tf_op jit(solution)/shard_map/local_late/pallas_call | solution.py:445
  29.2 3.1 %collective-permute-done.3 = f32[2,3,8,128]{3,2,1,0:T(8,128)S(1)} collective-permute-done((f32[2,3,8,128]{3,2,1,0:T(8,128)S(1)}, f32[2,3,8,128]{3,2,1,0:T(8,128)S(1)}, u32[]{:S(2)}, u32[]{:S(2)}) %collective-permute-start.3) | collective-permute-done | bytes 24608 | tf_op jit(solution)/shard_map/ppermute | solution.py:442
  32.3 0.0 collective-permute-done.2
  32.3 0.0 collective-permute-done.1
  32.3 0.0 collective-permute-done
  32.3 0.0 copy-start.4
  32.3 0.0 copy-start.5
  32.3 0.0 copy-start.6
  32.4 0.0 copy-start.7
  32.4 0.0 copy-start.8
  32.4 2.1 %all-gather.1 = f32[66,8,128]{2,1,0:T(8,128)S(1)} all-gather(f32[33,8,128]{2,1,0:T(8,128)S(1)} %pad_maximum_fusion), channel_id=3, replica_groups=mesh['x'=4,'z'=12,'core'=2,'lev'=8] {'core'}, dimensions={0}, use_global_device_ids=true | all-gather | bytes 405504 | tf_op jit(solution)/shard_map/all_gather | solution.py:454
  34.5 0.0 copy-done.4
  34.5 0.0 copy-done.5
  34.5 0.0 copy-done.6
  34.5 0.0 copy-done.7
  34.5 0.0 copy-done.8
  34.5 2.5 %finish.1 = (f32[2,3072]{1,0:T(2,128)}, f32[2,3072]{1,0:T(2,128)}, f32[2,1024]{1,0:T(2,128)}) custom-call(s32[1]{0:T(128)} %bitcast.core_ref, f32[2,18,8,128]{3,2,1,0:T(8,128)S(1)} %bitcast.16, f32[2,33,8,128]{3,2,1,0:T(8,128)S(1)} %bitcast.17, f32[24,6,8,128]{3,2,1,0:T(8,128)S(1)} %get-tuple-element.17.sums_ref, ...), custom_call_target="tpu_custom_call" | custom-call | tf_op jit(solution)/shard_map/finish/pallas_call | solution.py:455
  (8 shorter events, 0.0 us)
Async XLA Ops:
  0.6 3.9 %copy-start = (s32[10,3072]{1,0:T(8,128)S(1)}, s32[10,3072]{1,0:T(8,128)}, u32[]{:S(2)}) copy-start(s32[10,3072]{1,0:T(8,128)} %near_ref.5) | copy-start | bytes 368644
  0.7 3.9 %copy-start.1 = (f32[10,3072]{1,0:T(8,128)S(1)}, f32[10,3072]{1,0:T(8,128)}, u32[]{:S(2)}) copy-start(f32[10,3072]{1,0:T(8,128)} %weight_ref.5) | copy-start | bytes 368644
  7.1 25.2 %collective-permute-start = (f32[2,6,8,128]{3,2,1,0:T(8,128)S(1)}, f32[2,6,8,128]{3,2,1,0:T(8,128)S(1)}, u32[]{:S(2)}, u32[]{:S(2)}) collective-permute-start(f32[2,6,8,128]{3,2,1,0:T(8,128)S(1)} %slice_select_fusion), channel_id=1, source_target_pairs={{0,16},{16,32},{32,48},{48,64},{64,80},{80,96},{96,112},{112,128},... | collective-permute-start | bytes 147464 | tf_op jit(solution)/shard_map/ppermute | solution.py:430
  21.1 11.1 %collective-permute-start.2 = (f32[7,8,128]{2,1,0:T(8,128)S(1)}, f32[7,8,128]{2,1,0:T(8,128)S(1)}, u32[]{:S(2)}, u32[]{:S(2)}) collective-permute-start(f32[7,8,128]{2,1,0:T(8,128)S(1)} %pad_maximum_fusion.2), channel_id=1, source_target_pairs={{0,48},{16,64},{32,80},{48,96},{64,112},{80,128},{96,144},{112,160... | collective-permute-start | bytes 86024 | tf_op jit(solution)/shard_map/ppermute | solution.py:430
  23.3 5.3 %copy-start.2 = (s32[6,1024]{1,0:T(8,128)S(1)}, s32[6,1024]{1,0:T(8,128)}, u32[]{:S(2)}) copy-start(s32[6,1024]{1,0:T(8,128)} %cells_ref.3) | copy-start | bytes 73732
  23.4 5.3 %copy-start.3 = (f32[6,1024]{1,0:T(8,128)S(1)}, f32[6,1024]{1,0:T(8,128)}, u32[]{:S(2)}) copy-start(f32[6,1024]{1,0:T(8,128)} %share_ref.3) | copy-start | bytes 73732
  23.4 8.9 %collective-permute-start.1 = (f32[8,8,128]{2,1,0:T(8,128)S(1)}, f32[8,8,128]{2,1,0:T(8,128)S(1)}, u32[]{:S(2)}, u32[]{:S(2)}) collective-permute-start(f32[8,8,128]{2,1,0:T(8,128)S(1)} %pad_maximum_fusion.1), channel_id=1, source_target_pairs={{0,32},{16,48},{32,64},{48,80},{64,96},{80,112},{96,128},{112,144}... | collective-permute-start | bytes 98312 | tf_op jit(solution)/shard_map/ppermute | solution.py:430
  26.5 5.8 %collective-permute-start.3 = (f32[2,3,8,128]{3,2,1,0:T(8,128)S(1)}, f32[2,3,8,128]{3,2,1,0:T(8,128)S(1)}, u32[]{:S(2)}, u32[]{:S(2)}) collective-permute-start(f32[2,3,8,128]{3,2,1,0:T(8,128)S(1)} %slice_select_fusion.1), channel_id=1, source_target_pairs={{0,1},{1,2},{2,3},{3,4},{4,5},{5,6},{6,7},{9,8},{10,9},{11,10},{12... | collective-permute-start | bytes 73736 | tf_op jit(solution)/shard_map/ppermute | solution.py:442
  32.3 2.2 %copy-start.4 = (f32[2,3072]{1,0:T(2,128)S(1)}, f32[2,3072]{1,0:T(2,128)}, u32[]{:S(2)}) copy-start(f32[2,3072]{1,0:T(2,128)} %speed_ref.1) | copy-start | bytes 73732
  32.3 2.2 %copy-start.5 = (f32[2,3072]{1,0:T(2,128)S(1)}, f32[2,3072]{1,0:T(2,128)}, u32[]{:S(2)}) copy-start(f32[2,3072]{1,0:T(2,128)} %vort_ref.1) | copy-start | bytes 73732
  32.3 2.2 %copy-start.6 = (s32[2,3072]{1,0:T(2,128)S(1)}, s32[2,3072]{1,0:T(2,128)}, u32[]{:S(2)}) copy-start(s32[2,3072]{1,0:T(2,128)} %ends_ref.1) | copy-start | bytes 73732
  32.4 2.2 %copy-start.7 = (f32[2,3072]{1,0:T(2,128)S(1)}, f32[2,3072]{1,0:T(2,128)}, u32[]{:S(2)}) copy-start(f32[2,3072]{1,0:T(2,128)} %wind_ref.1) | copy-start | bytes 73732
  32.4 2.2 %copy-start.8 = (f32[3072]{0:T(1024)S(1)}, f32[3072]{0:T(1024)}, u32[]{:S(2)}) copy-start(f32[3072]{0:T(1024)} %param.23) | copy-start | bytes 36868

commit v6 on v5

--- a/solution.py
+++ b/solution.py
@@ -14,7 +14,7 @@
 WAY = 6
 RIM = 2 * WAY
 TILES = RIM + 6
-EARLY = 4
+EARLY = 3
 NEAR, MIDDLE, FAR, EDGE = 0, 12, 20, 27
 
 

time: 37.4 us -> 37.4 us (level)
  no operation moved by 1% of the time
where the time goes in v6:
time: 37.4 us; the launch traced here: 37.1 us
  starting transfers between devices  21.4 us (57%)
  Pallas kernels  7.24 us (19%)
  blocking collectives  4.37 us (12%)
  waiting for transfers between devices  3.14 us (8%)
  between operations  0.89 us (2%)
    ppermute x3, starting transfers between devices, apart(): return lax.ppermute(block, mesh_axes, right + left)  19.3 us
    ppermute x1, waiting for transfers between devices, body(): lax.ppermute(rims, ('core', 'lev'), up + down).reshape(6, 8, LANES)  3.13 us
    pallas_call x1, Pallas kernels, body(): pl.pallas_call(finish_kernel, out_shape=(jax.ShapeDtypeStruct(velocity.sh...  2.55 us
    pallas_call x1, Pallas kernels, body(): pl.pallas_call(local_early_kernel, out_shape=sums_shape, in_specs=[flag]...  2.49 us
    all_gather x1, blocking collectives, body(): own = lax.all_gather(sent, 'core')  2.23 us
    all_gather x1, blocking collectives, body(): around = lax.all_gather(arrived, 'core')  2.13 us
    ppermute x1, starting transfers between devices, body(): lax.ppermute(rims, ('core', 'lev'), up + down).reshape(6, 8, LANES)  2.08 us
    pallas_call x1, Pallas kernels, body(): pl.pallas_call(pack_kernel, out_shape=(jax.ShapeDtypeStruct((TILES, 8, LA...  1.67 us
  transfers between devices with their start and end apart: 4, of which 1 were waited for; matrix products, arithmetic and copies ran while one was open for 0% of the time, Pallas kernels for 1%

profile of v6, /device:TPU:25, one launch (start us, length us, event | category | flops | bytes accessed | tf_op | source)
XLA Modules:
  0.0 37.1 jit_solution(1051737192132099830)
XLA Ops:
  0.6 0.0 copy-start
  0.7 0.0 copy-start.1
  0.7 1.7 %pack.1 = (f32[18,8,128]{2,1,0:T(8,128)S(1)}, f32[18,8,128]{2,1,0:T(8,128)S(1)}) custom-call(f32[2,3072]{1,0:T(2,128)} %speed_ref.1, f32[2,3072]{1,0:T(2,128)} %height_hbm.1, f32[2,3072]{1,0:T(2,128)} %vort_ref.1, s32[6,128]{1,0:T(8,128)} %edge_list_hbm.1, s32[6,64]{1,0:T(8,128)} %cell_list_hbm.1, s32[6,1024]{1,0:T(8,128)} %cells_ref.3, f32[6,1024]{1,0:T(8,128)} %share_ref.3), custom_call_target="tpu_custom_call" | custom-call | tf_op jit(solution)/shard_map/pack/pallas_call | solution.py:390
  2.4 2.2 %all-gather = f32[36,8,128]{2,1,0:T(8,128)S(1)} all-gather(f32[18,8,128]{2,1,0:T(8,128)S(1)} %get-tuple-element.11), channel_id=2, replica_groups=mesh['x'=4,'z'=12,'core'=2,'lev'=8] {'core'}, dimensions={0}, use_global_device_ids=true | all-gather | bytes 221184 | tf_op jit(solution)/shard_map/all_gather | solution.py:405
  4.6 0.0 copy-done
  4.6 0.0 copy-done.1
  4.6 2.5 %local_early.1.made_ref = f32[24,6,8,128]{3,2,1,0:T(8,128)S(1)} custom-call(s32[1]{0:T(128)} %bitcast.2.early_ref, f32[18,8,128]{2,1,0:T(8,128)S(1)} %get-tuple-element.14.table_ref, s32[10,3072]{1,0:T(8,128)S(1)} %copy-done, f32[10,3072]{1,0:T(8,128)S(1)} %copy-done.1), custom_call_target="tpu_custom_call" | custom-call | tf_op jit(solution)/shard_map/local_early/pallas_call | solution.py:414
  7.1 14.0 %collective-permute-start = (f32[2,6,8,128]{3,2,1,0:T(8,128)S(1)}, f32[2,6,8,128]{3,2,1,0:T(8,128)S(1)}, u32[]{:S(2)}, u32[]{:S(2)}) collective-permute-start(f32[2,6,8,128]{3,2,1,0:T(8,128)S(1)} %slice_select_fusion), channel_id=1, source_target_pairs={{0,16},{16,32},{32,48},{48,64},{64,80},{80,96},{96,112},{112,128},... | collective-permute-start | bytes 147464 | tf_op jit(solution)/shard_map/ppermute | solution.py:430
  21.1 2.2 %collective-permute-start.2 = (f32[7,8,128]{2,1,0:T(8,128)S(1)}, f32[7,8,128]{2,1,0:T(8,128)S(1)}, u32[]{:S(2)}, u32[]{:S(2)}) collective-permute-start(f32[7,8,128]{2,1,0:T(8,128)S(1)} %pad_maximum_fusion.2), channel_id=1, source_target_pairs={{0,48},{16,64},{32,80},{48,96},{64,112},{80,128},{96,144},{112,160... | collective-permute-start | bytes 86024 | tf_op jit(solution)/shard_map/ppermute | solution.py:430
  23.3 0.0 copy-start.2
  23.4 0.0 copy-start.3
  23.4 3.1 %collective-permute-start.1 = (f32[8,8,128]{2,1,0:T(8,128)S(1)}, f32[8,8,128]{2,1,0:T(8,128)S(1)}, u32[]{:S(2)}, u32[]{:S(2)}) collective-permute-start(f32[8,8,128]{2,1,0:T(8,128)S(1)} %pad_maximum_fusion.1), channel_id=1, source_target_pairs={{0,32},{16,48},{32,64},{48,80},{64,96},{80,112},{96,128},{112,144}... | collective-permute-start | bytes 98312 | tf_op jit(solution)/shard_map/ppermute | solution.py:430
  26.5 2.1 %collective-permute-start.3 = (f32[2,3,8,128]{3,2,1,0:T(8,128)S(1)}, f32[2,3,8,128]{3,2,1,0:T(8,128)S(1)}, u32[]{:S(2)}, u32[]{:S(2)}) collective-permute-start(f32[2,3,8,128]{3,2,1,0:T(8,128)S(1)} %slice_select_fusion.1), channel_id=1, source_target_pairs={{0,1},{1,2},{2,3},{3,4},{4,5},{5,6},{6,7},{9,8},{10,9},{11,10},{12... | collective-permute-start | bytes 73736 | tf_op jit(solution)/shard_map/ppermute | solution.py:442
  28.6 0.0 copy-done.2
  28.6 0.0 copy-done.3
  28.6 0.5 %local_late.1 = (f32[24,6,8,128]{3,2,1,0:T(8,128)S(1)}, f32[8,2,8,128]{3,2,1,0:T(8,128)S(1)}) custom-call(s32[1]{0:T(128)} %bitcast.2.early_ref, f32[24,6,8,128]{3,2,1,0:T(8,128)S(1)} %local_early.1.made_ref, f32[18,8,128]{2,1,0:T(8,128)S(1)} %get-tuple-element.14.table_ref, s32[10,3072]{1,0:T(8,128)S(1)} %copy-done, f32[10,3072]{1,0:T(8,128)S(1)} %copy-done.1, ...), custom_call_target="tpu_custom_call" | custom-call | flops 20000000 | bytes 1000000 | tf_op jit(solution)/shard_map/local_late/pallas_call | solution.py:445
  29.2 3.1 %collective-permute-done.3 = f32[2,3,8,128]{3,2,1,0:T(8,128)S(1)} collective-permute-done((f32[2,3,8,128]{3,2,1,0:T(8,128)S(1)}, f32[2,3,8,128]{3,2,1,0:T(8,128)S(1)}, u32[]{:S(2)}, u32[]{:S(2)}) %collective-permute-start.3) | collective-permute-done | bytes 24608 | tf_op jit(solution)/shard_map/ppermute | solution.py:442
  32.3 0.0 collective-permute-done.2
  32.3 0.0 collective-permute-done.1
  32.3 0.0 collective-permute-done
  32.3 0.0 copy-start.4
  32.3 0.0 copy-start.5
  32.3 0.0 copy-start.6
  32.4 0.0 copy-start.7
  32.4 0.0 copy-start.8
  32.4 2.1 %all-gather.1 = f32[66,8,128]{2,1,0:T(8,128)S(1)} all-gather(f32[33,8,128]{2,1,0:T(8,128)S(1)} %pad_maximum_fusion), channel_id=3, replica_groups=mesh['x'=4,'z'=12,'core'=2,'lev'=8] {'core'}, dimensions={0}, use_global_device_ids=true | all-gather | bytes 405504 | tf_op jit(solution)/shard_map/all_gather | solution.py:454
  34.5 0.0 copy-done.4
  34.5 0.0 copy-done.5
  34.5 0.0 copy-done.6
  34.5 0.0 copy-done.7
  34.5 0.0 copy-done.8
  34.5 2.5 %finish.1 = (f32[2,3072]{1,0:T(2,128)}, f32[2,3072]{1,0:T(2,128)}, f32[2,1024]{1,0:T(2,128)}) custom-call(s32[1]{0:T(128)} %bitcast.core_ref, f32[2,18,8,128]{3,2,1,0:T(8,128)S(1)} %bitcast.16, f32[2,33,8,128]{3,2,1,0:T(8,128)S(1)} %bitcast.17, f32[24,6,8,128]{3,2,1,0:T(8,128)S(1)} %get-tuple-element.17.sums_ref, ...), custom_call_target="tpu_custom_call" | custom-call | tf_op jit(solution)/shard_map/finish/pallas_call | solution.py:455
  (8 shorter events, 0.0 us)
Async XLA Ops:
  0.6 3.9 %copy-start = (s32[10,3072]{1,0:T(8,128)S(1)}, s32[10,3072]{1,0:T(8,128)}, u32[]{:S(2)}) copy-start(s32[10,3072]{1,0:T(8,128)} %near_ref.5) | copy-start | bytes 368644
  0.7 3.9 %copy-start.1 = (f32[10,3072]{1,0:T(8,128)S(1)}, f32[10,3072]{1,0:T(8,128)}, u32[]{:S(2)}) copy-start(f32[10,3072]{1,0:T(8,128)} %weight_ref.5) | copy-start | bytes 368644
  7.1 25.2 %collective-permute-start = (f32[2,6,8,128]{3,2,1,0:T(8,128)S(1)}, f32[2,6,8,128]{3,2,1,0:T(8,128)S(1)}, u32[]{:S(2)}, u32[]{:S(2)}) collective-permute-start(f32[2,6,8,128]{3,2,1,0:T(8,128)S(1)} %slice_select_fusion), channel_id=1, source_target_pairs={{0,16},{16,32},{32,48},{48,64},{64,80},{80,96},{96,112},{112,128},... | collective-permute-start | bytes 147464 | tf_op jit(solution)/shard_map/ppermute | solution.py:430
  21.1 11.1 %collective-permute-start.2 = (f32[7,8,128]{2,1,0:T(8,128)S(1)}, f32[7,8,128]{2,1,0:T(8,128)S(1)}, u32[]{:S(2)}, u32[]{:S(2)}) collective-permute-start(f32[7,8,128]{2,1,0:T(8,128)S(1)} %pad_maximum_fusion.2), channel_id=1, source_target_pairs={{0,48},{16,64},{32,80},{48,96},{64,112},{80,128},{96,144},{112,160... | collective-permute-start | bytes 86024 | tf_op jit(solution)/shard_map/ppermute | solution.py:430
  23.3 5.3 %copy-start.2 = (s32[6,1024]{1,0:T(8,128)S(1)}, s32[6,1024]{1,0:T(8,128)}, u32[]{:S(2)}) copy-start(s32[6,1024]{1,0:T(8,128)} %cells_ref.3) | copy-start | bytes 73732
  23.4 5.3 %copy-start.3 = (f32[6,1024]{1,0:T(8,128)S(1)}, f32[6,1024]{1,0:T(8,128)}, u32[]{:S(2)}) copy-start(f32[6,1024]{1,0:T(8,128)} %share_ref.3) | copy-start | bytes 73732
  23.4 8.9 %collective-permute-start.1 = (f32[8,8,128]{2,1,0:T(8,128)S(1)}, f32[8,8,128]{2,1,0:T(8,128)S(1)}, u32[]{:S(2)}, u32[]{:S(2)}) collective-permute-start(f32[8,8,128]{2,1,0:T(8,128)S(1)} %pad_maximum_fusion.1), channel_id=1, source_target_pairs={{0,32},{16,48},{32,64},{48,80},{64,96},{80,112},{96,128},{112,144}... | collective-permute-start | bytes 98312 | tf_op jit(solution)/shard_map/ppermute | solution.py:430
  26.5 5.8 %collective-permute-start.3 = (f32[2,3,8,128]{3,2,1,0:T(8,128)S(1)}, f32[2,3,8,128]{3,2,1,0:T(8,128)S(1)}, u32[]{:S(2)}, u32[]{:S(2)}) collective-permute-start(f32[2,3,8,128]{3,2,1,0:T(8,128)S(1)} %slice_select_fusion.1), channel_id=1, source_target_pairs={{0,1},{1,2},{2,3},{3,4},{4,5},{5,6},{6,7},{9,8},{10,9},{11,10},{12... | collective-permute-start | bytes 73736 | tf_op jit(solution)/shard_map/ppermute | solution.py:442
  32.3 2.2 %copy-start.4 = (f32[2,3072]{1,0:T(2,128)S(1)}, f32[2,3072]{1,0:T(2,128)}, u32[]{:S(2)}) copy-start(f32[2,3072]{1,0:T(2,128)} %speed_ref.1) | copy-start | bytes 73732
  32.3 2.2 %copy-start.5 = (f32[2,3072]{1,0:T(2,128)S(1)}, f32[2,3072]{1,0:T(2,128)}, u32[]{:S(2)}) copy-start(f32[2,3072]{1,0:T(2,128)} %vort_ref.1) | copy-start | bytes 73732
  32.3 2.2 %copy-start.6 = (s32[2,3072]{1,0:T(2,128)S(1)}, s32[2,3072]{1,0:T(2,128)}, u32[]{:S(2)}) copy-start(s32[2,3072]{1,0:T(2,128)} %ends_ref.1) | copy-start | bytes 73732
  32.4 2.2 %copy-start.7 = (f32[2,3072]{1,0:T(2,128)S(1)}, f32[2,3072]{1,0:T(2,128)}, u32[]{:S(2)}) copy-start(f32[2,3072]{1,0:T(2,128)} %wind_ref.1) | copy-start | bytes 73732
  32.4 2.2 %copy-start.8 = (f32[3072]{0:T(1024)S(1)}, f32[3072]{0:T(1024)}, u32[]{:S(2)}) copy-start(f32[3072]{0:T(1024)} %param.23) | copy-start | bytes 36868
